TPU v7x, 32 devices: a whole 2x2x4 slice. The times are simulated.
32 devices in a mesh: row: 8 (over y, x, core), col: 4 (over z).
Axes of the slice: x: 2, y: 2, z: 4, core: 2. Of those that a mesh axis runs over, the one named last changes fastest.
Arguments:
- points: float32 [8, 4096], P(None, ('row', 'col')), may hold values from -1.8 to 1.8
- inverse_scale: float32 [8], replicated, may hold values from 0.5 to 1
- targets: float32 [16, 4096], P(None, ('row', 'col')), may hold values from -3.5 to 5.5
- noise_var: float32 [16], replicated, may hold values from 0.5 to 2
Outputs:
- solution: float32 [16, 4096], P(None, ('row', 'col'))
- residual: float32 [16, 4096], P(None, ('row', 'col'))
All inputs are finite; a program needn't handle non-finite values.
Results may differ from a plain program's by a relative error of at most 0.0015.
Values sent between devices are 32-bit elements; how exact they have to be, the bound alone decides.
A program may use at most 64 MiB of HBM per device.

v0:
```python
import jax
import jax.numpy as jnp
from jax import lax
from jax.sharding import PartitionSpec as P

ITERS = 2


exact_mode = lax.Precision.HIGHEST


def block_terms(row_z, row_half, col_z, col_v):
    col_half = 0.5 * jnp.sum(col_z * col_z, axis=0)
    inner_products = jnp.einsum("fb,fr->br", col_z, row_z, precision=exact_mode)
    kernel = jnp.exp(inner_products - col_half[:, None] - row_half[None, :])
    return jnp.dot(col_v, kernel, precision=exact_mode, preferred_element_type=jnp.float32)


def slab_width(row_count, column_count):
    block_cols = max(128, 1048576 // row_count)
    if column_count > block_cols and column_count % block_cols == 0:
        return block_cols
    return column_count


def kernel_terms(row_z, row_half, col_z, col_v):
    column_count = col_z.shape[1]
    block_cols = slab_width(row_z.shape[1], column_count)
    if block_cols < column_count:
        block_count = column_count // block_cols
        z_slabs = col_z.reshape(col_z.shape[0], block_count, block_cols).transpose(1, 0, 2)
        v_slabs = col_v.reshape(col_v.shape[0], block_count, block_cols).transpose(1, 0, 2)

        def advance(accumulated, slabs):
            return (accumulated + block_terms(row_z, row_half, slabs[0], slabs[1]), None)

        initial = jnp.zeros((col_v.shape[0], row_z.shape[1]), jnp.float32)
        accumulated, unused = lax.scan(advance, initial, (z_slabs, v_slabs))
        return accumulated
    return block_terms(row_z, row_half, col_z, col_v)


def squares(residual):
    return lax.psum(jnp.sum(residual * residual, axis=1), ("row", "col"))


def on_device(points, inverse_scale, targets, noise_var):
    scaled = points * inverse_scale[:, None]
    all_scaled = lax.all_gather(scaled, ("row", "col"), axis=1, tiled=True)
    row_half = 0.5 * jnp.sum(scaled * scaled, axis=0)
    solution = jnp.zeros_like(targets)
    residual = targets
    direction = targets
    norm_now = squares(residual)
    for turn in range(ITERS):
        image = (
            kernel_terms(
                scaled,
                row_half,
                all_scaled,
                lax.all_gather(direction, ("row", "col"), axis=1, tiled=True),
            )
            + noise_var[:, None] * direction
        )
        curvature = lax.psum(jnp.sum(direction * image, axis=1), ("row", "col"))
        step_size = norm_now / curvature
        solution = solution + step_size[:, None] * direction
        residual = residual - step_size[:, None] * image
        norm_next = squares(residual)
        direction = residual + (norm_next / norm_now)[:, None] * direction
        norm_now = norm_next
    return (solution, residual)


def solution(mesh):
    return jax.shard_map(
        on_device,
        mesh=mesh,
        in_specs=(P(None, ("row", "col")), P(), P(None, ("row", "col")), P()),
        out_specs=(P(None, ("row", "col")), P(None, ("row", "col"))),
        check_vma=False,
    )
```

profile of v0, /device:TPU:0, one launch (start us, length us, event | category | flops | bytes accessed | tf_op | source)
XLA Modules:
  0.0 329.1 jit_solution(10728062127517757069)
XLA Ops:
  0.6 0.0 copy-start
  0.6 0.0 copy-start.1
  0.7 0.8 multiply_reduce_fusion.5
  1.4 70.7 %all_gather.9 = f32[8,4096]{1,0:T(8,128)S(1)} all-gather(f32[8,128]{1,0:T(8,128)S(1)} %get-tuple-element.7), channel_id=1, replica_groups=mesh['row'=8,'col'=4] {'row','col'}, dimensions={1}, use_global_device_ids=true | all-gather | bytes 135168 | tf_op jit(solution)/shard_map/all_gather | solution.py:49
  72.2 3.9 %fusion.1 = f32[4096,128]{1,0:T(8,128)S(1)} fusion(f32[8,4096]{1,0:T(8,128)S(1)} %all_gather.9, f32[8,128]{1,0:T(8,128)S(1)} %get-tuple-element.7, f32[128]{0:T(128)S(1)} %broadcast_multiply_fusion.2, f32[4096]{0:T(1024)S(1)} %broadcast_multiply_fusion), kind=kOutput, calls=%fused_computation.2 | convolution fusion | flops 51380224 | bytes 2249216 | tf_op jit(solution)/shard_map/fb,fr->br/dot_general | solution.py:14
  76.1 0.0 copy-done
  76.1 65.4 %all_gather.10 = f32[16,4096]{1,0:T(8,128)S(1)} all-gather(f32[16,128]{1,0:T(8,128)S(1)} %copy-done), channel_id=1, replica_groups=mesh['row'=8,'col'=4] {'row','col'}, dimensions={1}, use_global_device_ids=true | all-gather | bytes 270336 | tf_op jit(solution)/shard_map/all_gather | solution.py:61
  141.5 0.0 copy-done.1
  141.5 1.4 multiply_reduce_fusion.3
  142.9 39.9 %all-reduce = (f32[16]{0:T(128)S(1)}, f32[16]{0:T(128)S(1)}) all-reduce(f32[16]{0:T(128)S(1)} %get-tuple-element.3, f32[16]{0:T(128)S(1)} %get-tuple-element.2), channel_id=1, replica_groups=mesh['row'=8,'col'=4] {'row','col'}, use_global_device_ids=true, to_apply=%region_1.0 | all-reduce | flops 32 | bytes 256 | tf_op jit(solution)/shard_map/psum | solution.py:44
  182.8 0.2 multiply_reduce_fusion.2
  182.9 38.4 %psum.30 = f32[16]{0:T(128)S(1)} all-reduce(f32[16]{0:T(128)S(1)} %multiply_reduce_fusion.2), channel_id=1, replica_groups=mesh['row'=8,'col'=4] {'row','col'}, use_global_device_ids=true, to_apply=%region_7.0 | all-reduce | flops 16 | bytes 128 | tf_op jit(solution)/shard_map/psum | solution.py:44
  221.4 0.1 multiply_add_fusion.1
  221.5 67.5 %all_gather.11 = f32[16,4096]{1,0:T(8,128)S(1)} all-gather(f32[16,128]{1,0:T(8,128)S(1)} %multiply_add_fusion.1), channel_id=1, replica_groups=mesh['row'=8,'col'=4] {'row','col'}, dimensions={1}, use_global_device_ids=true | all-gather | bytes 270336 | tf_op jit(solution)/shard_map/all_gather | solution.py:61
  289.0 1.3 multiply_reduce_fusion.1
  290.2 38.2 %psum.31 = f32[16]{0:T(128)S(1)} all-reduce(f32[16]{0:T(128)S(1)} %get-tuple-element.11), channel_id=1, replica_groups=mesh['row'=8,'col'=4] {'row','col'}, use_global_device_ids=true, to_apply=%region_9.0 | all-reduce | flops 16 | bytes 128 | tf_op jit(solution)/shard_map/psum | solution.py:65
  328.4 0.7 multiply_subtract_fusion
  (6 shorter events, 0.1 us)
Async XLA Ops:
  0.6 75.4 %copy-start = (f32[16,128]{1,0:T(8,128)S(1)}, f32[16,128]{1,0:T(8,128)}, u32[]{:S(2)}) copy-start(f32[16,128]{1,0:T(8,128)} %param.6) | copy-start | bytes 24580
  0.6 140.9 %copy-start.1 = (f32[16]{0:T(128)S(1)}, f32[16]{0:T(128)}, u32[]{:S(2)}) copy-start(f32[16]{0:T(128)} %param.7) | copy-start | bytes 196
where the time goes:
time: 330 us; the launch traced here: 329 us
  blocking collectives  320 us (97%)
  matrix products  6.48 us (2%)
    all_gather x2, blocking collectives, on_device(): lax.all_gather(direction, ('row', 'col'), axis=1, tiled=True)  133 us
    psum x2, blocking collectives, squares(): return lax.psum(jnp.sum(residual * residual, axis=1), ('row', 'col'))  78.3 us
    all_gather x1, blocking collectives, on_device(): all_scaled = lax.all_gather(scaled, ('row', 'col'), axis=1, tiled=True)  70.7 us
    psum x1, blocking collectives, on_device(): curvature = lax.psum(jnp.sum(direction * image, axis=1), ('row', 'col'))  38.2 us

commit v1 on v0

v1 whole, which is shorter than its diff:
```python
import functools
import math
import jax
import jax.numpy as jnp
from jax import lax
from jax.experimental import pallas as pl
from jax.experimental.pallas import tpu as pltpu
from jax.sharding import PartitionSpec as P

MESH = pl.DeviceIdType.MESH
ROOT = math.sqrt(1.0 / math.log(2.0))


def loop(low, high, body):
    if high - low <= 32:
        for k in range(low, high):
            body(k)
    else:

        def step(k, carry):
            body(k)
            return carry

        lax.fori_loop(low, high, step, 0)


def three(x):
    high = x.astype(jnp.bfloat16).astype(jnp.float32)
    rest = x - high
    middle = rest.astype(jnp.bfloat16).astype(jnp.float32)
    return high, middle, rest - middle


def two(x):
    high = x.astype(jnp.bfloat16)
    low = (x - high.astype(jnp.float32)).astype(jnp.bfloat16)
    return jnp.concatenate([high, low], axis=0)


def factors(z, left):
    z = z * ROOT
    half = 0.5 * jnp.sum(z * z, axis=0, keepdims=True)
    h, m, l = three(z)
    a, b, c = three(-half)
    row = lax.broadcasted_iota(jnp.int32, z.shape, 0)
    norms = jnp.where(row == 0, a, jnp.where(row == 1, b, jnp.where(row == 2, c, 0.0)))
    ones = jnp.ones_like(z)
    parts = [h, h, m, h, l, m, norms, ones] if left else [h, m, h, l, h, m, ones, norms]
    return jnp.concatenate(parts, axis=0).astype(jnp.bfloat16)


def column(ref, count, lanes):
    row = lax.broadcasted_iota(jnp.int32, (count, lanes), 0)
    out = jnp.zeros((count, lanes), jnp.float32)
    for k in range(count):
        out = jnp.where(row == k, ref[k], out)
    return out


def lane_sums(parts):
    used = sum(p.shape[0] for p in parts)
    parts = parts + [jnp.zeros((128 - used, 128), jnp.float32)]
    return jnp.sum(jnp.concatenate(parts, axis=0).T, axis=0, keepdims=True)


def to_column(row):
    return jnp.broadcast_to(row, (128, 128)).T


def kernel(
    nr, nc, feats, rhs, lanes,
    points_ref, scale_ref, targets_ref, noise_ref,
    solution_ref, residual_ref,
    raw, plane, line, part, wplane, wline, part2, tiny, tiny2, khi, klo,
    load_sem, send_sem, recv_p, recv_l, recv_part, recv_wp, recv_wl, recv_part2, recv_tiny, recv_tiny2,
):
    r, c = lax.axis_index("row"), lax.axis_index("col")
    every = nr * nc

    def at(kr, kc):
        return (lax.rem(r + kr, nr), lax.rem(c + kc, nc))

    load_points = pltpu.make_async_copy(points_ref, raw, load_sem.at[0])
    load_targets = pltpu.make_async_copy(targets_ref, plane.at[0, pl.ds(feats, rhs)], load_sem.at[1])
    load_points.start()
    load_targets.start()
    barrier = pltpu.get_barrier_semaphore()
    loop(1, nr, lambda k: pl.semaphore_signal(barrier, inc=1, device_id=at(k, 0), device_id_type=MESH))
    loop(1, nc, lambda k: pl.semaphore_signal(barrier, inc=1, device_id=at(0, k), device_id_type=MESH))
    scale = column(scale_ref, feats, lanes)
    noise = column(noise_ref, rhs, lanes)
    load_points.wait()
    plane[0, 0:feats, :] = raw[...] * scale
    load_targets.wait()
    line[0] = plane[0]
    pl.semaphore_wait(barrier, nr + nc - 2)

    def send(src, dst, slot, recv, device):
        return pltpu.make_async_remote_copy(
            src_ref=src, dst_ref=dst, send_sem=send_sem.at[slot], recv_sem=recv,
            device_id=device, device_id_type=MESH,
        )

    base = [0]

    def group(low, high, make):
        start = base[0]
        base[0] += high - low

        def copy(k):
            return make(k, start + k - low)

        return low, high, copy

    def begin(g):
        loop(g[0], g[1], lambda k: g[2](k).start())

    def arrived(g):
        loop(g[0], g[1], lambda k: g[2](k).wait_recv())

    def sent(g):
        loop(g[0], g[1], lambda k: g[2](k).wait_send())

    to_line = group(1, nc, lambda k, s: send(line.at[0], line.at[k], s, recv_l.at[k], at(0, k)))
    to_plane = group(1, nr, lambda k, s: send(plane.at[0], plane.at[k], s, recv_p.at[k], at(k, 0)))
    begin(to_line)
    begin(to_plane)

    arrived(to_line)
    right = factors(jnp.concatenate([line[k, 0:feats, :] for k in range(nc)], axis=1), False)
    arrived(to_plane)

    pair = 2 if nr % 2 == 0 else 1
    depth = pair * lanes

    def first(step, total):
        z = jnp.concatenate([plane[step * pair + k, 0:feats, :] for k in range(pair)], axis=1)
        v = jnp.concatenate([plane[step * pair + k, feats : feats + rhs, :] for k in range(pair)], axis=1)
        power = lax.dot_general(
            factors(z, True), right, (((0,), (0,)), ((), ())), preferred_element_type=jnp.float32
        )
        tile = jnp.exp2(power)
        high = tile.astype(jnp.bfloat16)
        low = (tile - high.astype(jnp.float32)).astype(jnp.bfloat16)
        khi[step] = high
        klo[step] = low
        v = two(v)
        both = jnp.dot(v, high, preferred_element_type=jnp.float32)
        return total + both[:rhs] + both[rhs:] + jnp.dot(v, low, preferred_element_type=jnp.float32)[:rhs]

    def steps(body):
        total = jnp.zeros((rhs, nc * lanes), jnp.float32)
        if nr // pair <= 8:
            for step in range(nr // pair):
                total = body(step, total)
            return total
        return lax.fori_loop(0, nr // pair, body, total)

    partial = steps(first)
    for k in range(nc):
        part[nc + k] = partial[:, k * lanes : (k + 1) * lanes]
    give = group(1, nc, lambda k, s: send(part.at[nc + k], part.at[k], s, recv_part.at[k], at(0, nc - k)))
    begin(give)
    target = plane[0, feats : feats + rhs, :]
    image = part[nc] + noise * target
    arrived(give)
    for k in range(1, nc):
        image = image + part[k]

    wplane[0] = image
    wline[0] = image
    w_line = group(1, nc, lambda k, s: send(wline.at[0], wline.at[k], s, recv_wl.at[k], at(0, k)))
    w_plane = group(1, nr, lambda k, s: send(wplane.at[0], wplane.at[k], s, recv_wp.at[k], at(k, 0)))
    begin(w_line)
    begin(w_plane)
    tiny[0] = lane_sums([target * target, target * image, image * image])

    def spread(ref, recv):
        def make(k, s):
            return send(ref.at[0], ref.at[k], s, recv.at[k], at(k // nc, lax.rem(k, nc)))

        return group(1, every, make)

    scalars = spread(tiny, recv_tiny)
    begin(scalars)
    arrived(w_line)
    arrived(w_plane)
    arrived(scalars)

    sums = to_column(jnp.sum(tiny[...], axis=0))
    tt, tw, ww = sums[:rhs], sums[rhs : 2 * rhs], sums[2 * rhs : 3 * rhs]
    alpha = tt / tw
    beta = alpha * alpha * ww / tt - 1.0

    def direct(t, w):
        return (t - alpha * w) + beta * t

    def second(step, total):
        v = two(jnp.concatenate(
            [direct(plane[step * pair + k, feats : feats + rhs, :], wplane[step * pair + k]) for k in range(pair)],
            axis=1,
        ))
        both = jnp.dot(v, khi[step], preferred_element_type=jnp.float32)
        return total + both[:rhs] + both[rhs:] + jnp.dot(v, klo[step], preferred_element_type=jnp.float32)[:rhs]

    partial = steps(second)
    for k in range(nc):
        part2[nc + k] = partial[:, k * lanes : (k + 1) * lanes]
    give2 = group(1, nc, lambda k, s: send(part2.at[nc + k], part2.at[k], s, recv_part2.at[k], at(0, nc - k)))
    begin(give2)
    residual = target - alpha * image
    direction = direct(target, image)
    curved = noise * direction * direction
    for k in range(nc):
        curved = curved + direct(line[k, feats : feats + rhs, :], wline[k]) * partial[:, k * lanes : (k + 1) * lanes]
    tiny2[0] = lane_sums([curved, residual * residual])
    scalars2 = spread(tiny2, recv_tiny2)
    begin(scalars2)
    image2 = part2[nc] + noise * direction
    arrived(give2)
    for k in range(1, nc):
        image2 = image2 + part2[k]
    arrived(scalars2)
    sums = to_column(jnp.sum(tiny2[...], axis=0))
    alpha2 = sums[rhs : 2 * rhs] / sums[:rhs]
    solution_ref[...] = alpha * target + alpha2 * direction
    residual_ref[...] = residual - alpha2 * image2
    for g in (to_line, to_plane, give, w_line, w_plane, scalars, give2, scalars2):
        sent(g)


def solution(mesh):
    nr, nc = mesh.shape["row"], mesh.shape["col"]

    def on_device(points, inverse_scale, targets, noise_var):
        feats, lanes = points.shape
        rhs = targets.shape[0]
        pair = 2 if nr % 2 == 0 else 1
        every = nr * nc
        f32 = jnp.float32
        block = jax.ShapeDtypeStruct((rhs, lanes), f32)
        dma = pltpu.SemaphoreType.DMA
        sends = 4 * (nc - 1) + 2 * (nr - 1) + 2 * (every - 1)
        return pl.pallas_call(
            functools.partial(kernel, nr, nc, feats, rhs, lanes),
            out_shape=(block, block),
            in_specs=[
                pl.BlockSpec(memory_space=pl.ANY),
                pl.BlockSpec(memory_space=pltpu.SMEM),
                pl.BlockSpec(memory_space=pl.ANY),
                pl.BlockSpec(memory_space=pltpu.SMEM),
            ],
            out_specs=(pl.BlockSpec(memory_space=pltpu.VMEM),) * 2,
            scratch_shapes=[
                pltpu.VMEM((feats, lanes), f32),
                pltpu.VMEM((nr, feats + rhs, lanes), f32),
                pltpu.VMEM((nc, feats + rhs, lanes), f32),
                pltpu.VMEM((2 * nc, rhs, lanes), f32),
                pltpu.VMEM((nr, rhs, lanes), f32),
                pltpu.VMEM((nc, rhs, lanes), f32),
                pltpu.VMEM((2 * nc, rhs, lanes), f32),
                pltpu.VMEM((every, 1, lanes), f32),
                pltpu.VMEM((every, 1, lanes), f32),
                pltpu.VMEM((nr // pair, pair * lanes, nc * lanes), jnp.bfloat16),
                pltpu.VMEM((nr // pair, pair * lanes, nc * lanes), jnp.bfloat16),
                dma((2,)),
                dma((sends,)),
                dma((nr,)),
                dma((nc,)),
                dma((nc,)),
                dma((nr,)),
                dma((nc,)),
                dma((nc,)),
                dma((every,)),
                dma((every,)),
            ],
            compiler_params=pltpu.CompilerParams(
                collective_id=0, has_side_effects=True, vmem_limit_bytes=56 * 1024 * 1024
            ),
        )(points, inverse_scale, targets, noise_var)

    spec = P(None, ("row", "col"))
    return jax.shard_map(
        on_device, mesh=mesh, in_specs=(spec, P(), spec, P()), out_specs=(spec, spec), check_vma=False
    )
```

time: 330 us -> 30 us (0.09)
  blocking collectives: 320 us -> 0 us
  Pallas kernels: 0 us -> 27.2 us
  matrix products: 6.48 us -> 0 us
    all_gather x3 -> x0, blocking collectives: 204 us -> none  [the longest x2 133 us: on_device(): lax.all_gather(direction, ('row', 'col'), axis=1, tiled=True)]
    psum x3 -> x0, blocking collectives: 116 us -> none  [the longest x2 78.3 us: squares(): return lax.psum(jnp.sum(residual * residual, axis=1), ('row', 'col'))]
    pallas_call x0 -> x1, Pallas kernels: none -> 27.2 us  [on_device(): pl.pallas_call(functools.partial(kernel, nr, nc, feats, rhs, lanes), out_...]
    dot_general x3 -> x0, matrix products: 6.48 us -> none  [the longest x1 3.88 us: block_terms(): inner_products = jnp.einsum('fb,fr->br', col_z, row_z, precision=exact_mode)]
where the time goes in v1:
time: 30 us; the launch traced here: 29.7 us
  Pallas kernels  27.2 us (91%)
  local copies, waits for them, and re-layouts  1.9 us (6%)
  between operations  0.65 us (2%)
    pallas_call x1, Pallas kernels, on_device(): pl.pallas_call(functools.partial(kernel, nr, nc, feats, rhs, lanes), out_...  27.2 us
    unnamed x4, local copies, waits for them, and re-layouts  1.9 us

profile of v1, /device:TPU:0, one launch (start us, length us, event | category | flops | bytes accessed | tf_op | source)
XLA Modules:
  0.0 29.7 jit_solution(13963678259193651440)
XLA Ops:
  0.6 27.2 %shard_map.59 = (f32[16,128]{1,0:T(8,128)}, f32[16,128]{1,0:T(8,128)}) custom-call(f32[8,128]{1,0:T(8,128)} %points_ref.1, f32[8]{0:T(128)} %scale_ref.1, f32[16,128]{1,0:T(8,128)} %targets_ref.1, f32[16]{0:T(128)} %noise_ref.1), custom_call_target="tpu_custom_call" | custom-call | tf_op jit(solution)/shard_map/pallas_call | solution.py:244
  27.8 0.0 copy-start
  27.8 1.3 %copy.8 = f32[16,128]{1,0:T(8,128)} copy(f32[16,128]{1,0:T(8,128)} %get-tuple-element.4) | data formatting | bytes 16384
  29.1 0.0 copy-done
  29.1 0.6 %copy.9 = f32[16,128]{1,0:T(8,128)} copy(f32[16,128]{1,0:T(8,128)S(1)} %copy-done) | data formatting | bytes 16384
Async XLA Ops:
  27.8 1.3 %copy-start = (f32[16,128]{1,0:T(8,128)S(1)}, f32[16,128]{1,0:T(8,128)}, u32[]{:S(2)}) copy-start(f32[16,128]{1,0:T(8,128)} %get-tuple-element.5) | copy-start | bytes 24580

commit v2 on v1

v2 whole, which is shorter than its diff:
```python
import functools
import math
import jax
import jax.numpy as jnp
from jax import lax
from jax.experimental import pallas as pl
from jax.experimental.pallas import tpu as pltpu
from jax.sharding import PartitionSpec as P

MESH = pl.DeviceIdType.MESH
ROOT = math.sqrt(1.0 / math.log(2.0))


def loop(low, high, body):
    if high - low <= 32:
        for k in range(low, high):
            body(k)
    else:

        def step(k, carry):
            body(k)
            return carry

        lax.fori_loop(low, high, step, 0)


def three(x):
    high = x.astype(jnp.bfloat16).astype(jnp.float32)
    rest = x - high
    middle = rest.astype(jnp.bfloat16).astype(jnp.float32)
    return high, middle, rest - middle


def two(x):
    high = x.astype(jnp.bfloat16)
    low = (x - high.astype(jnp.float32)).astype(jnp.bfloat16)
    return jnp.concatenate([high, low], axis=0)


def factors(z, left):
    z = z * ROOT
    half = 0.5 * jnp.sum(z * z, axis=0, keepdims=True)
    h, m, l = three(z)
    a, b, c = three(-half)
    row = lax.broadcasted_iota(jnp.int32, z.shape, 0)
    norms = jnp.where(row == 0, a, jnp.where(row == 1, b, jnp.where(row == 2, c, 0.0)))
    ones = jnp.ones_like(z)
    parts = [h, h, m, h, l, m, norms, ones] if left else [h, m, h, l, h, m, ones, norms]
    return jnp.concatenate(parts, axis=0)


def column(ref, count, lanes):
    row = lax.broadcasted_iota(jnp.int32, (count, lanes), 0)
    out = jnp.zeros((count, lanes), jnp.float32)
    for k in range(count):
        out = jnp.where(row == k, ref[k], out)
    return out


def lane_sums(parts):
    used = sum(p.shape[0] for p in parts)
    parts = parts + [jnp.zeros((128 - used, 128), jnp.float32)]
    return jnp.sum(jnp.concatenate(parts, axis=0).T, axis=0, keepdims=True)


def to_column(row):
    return jnp.broadcast_to(row, (128, 128)).T


def kernel(
    nr, nc, feats, rhs, lanes,
    points_ref, scale_in, targets_ref, noise_in,
    solution_ref, residual_ref,
    raw, scale_ref, noise_ref, plane, line, part, wplane, wline, part2, tiny, tiny2, khi, klo,
    load_sem, send_sem, recv_sem,
):
    r, c = lax.axis_index("row"), lax.axis_index("col")
    every = nr * nc

    def at(kr, kc):
        return (lax.rem(r + kr, nr), lax.rem(c + kc, nc))

    barrier = pltpu.get_barrier_semaphore()
    loop(1, nr, lambda k: pl.semaphore_signal(barrier, inc=1, device_id=at(k, 0), device_id_type=MESH))
    loop(1, nc, lambda k: pl.semaphore_signal(barrier, inc=1, device_id=at(0, k), device_id_type=MESH))
    own = pl.ds(feats, rhs)
    loads = [
        pltpu.make_async_copy(src, dst, load_sem.at[i])
        for i, (src, dst) in enumerate([
            (points_ref, raw), (scale_in, scale_ref), (targets_ref, plane.at[0, own]),
            (targets_ref, line.at[0, own]), (noise_in, noise_ref),
        ])
    ]
    for load in loads:
        load.start()
    loads[0].wait()
    loads[1].wait()
    scaled = raw[...] * column(scale_ref, feats, lanes)
    plane[0, 0:feats, :] = scaled
    line[0, 0:feats, :] = scaled
    for load in loads[2:]:
        load.wait()
    pl.semaphore_wait(barrier, nr + nc - 2)

    class Group:
        count = 0

        def __init__(self, ref, last, peer, src=lambda k: 0):
            self.ref, self.last, self.peer, self.src = ref, last, peer, src
            self.sem = Group.count
            Group.count += 1

        def start(self, low=1, high=None):
            def one(k):
                pltpu.make_async_remote_copy(
                    src_ref=self.ref.at[self.src(k)], dst_ref=self.ref.at[k],
                    send_sem=send_sem.at[self.sem], recv_sem=recv_sem.at[self.sem],
                    device_id=self.peer(k), device_id_type=MESH,
                ).start()

            loop(low, self.last if high is None else high, one)

        def wait(self, sem):
            slots = self.ref.at[pl.ds(1, self.last - 1)]
            pltpu.make_async_copy(slots, slots, sem.at[self.sem]).wait()

        def arrived(self):
            self.wait(recv_sem)

        def sent(self):
            self.wait(send_sem)

    along_col = lambda k: at(0, k)
    along_row = lambda k: at(k, 0)
    back_col = lambda k: at(0, nc - k)
    anywhere = lambda k: at(k // nc, lax.rem(k, nc))
    to_line = Group(line, nc, along_col)
    to_plane = Group(plane, nr, along_row)
    give = Group(part, nc, back_col, lambda k: nc + k)
    w_line = Group(wline, nc, along_col)
    w_plane = Group(wplane, nr, along_row)
    scalars = Group(tiny, every, anywhere)
    give2 = Group(part2, nc, back_col, lambda k: nc + k)
    scalars2 = Group(tiny2, every, anywhere)

    to_line.start()
    to_plane.start()

    pair = 2 if nr % 2 == 0 else 1
    steps = nr // pair
    wide = 2 if nc % 2 == 0 else 1
    order = list(range(1, nc)) + [0]
    order = [order[i : i + wide] for i in range(0, nc, wide)]
    few = steps <= 8

    def cached(make):
        held = {}

        def get(step):
            if not few:
                return make(step)
            if step not in held:
                held[step] = make(step)
            return held[step]

        return get

    def total(body):
        out = jnp.zeros((rhs, wide * lanes), jnp.float32)
        if few:
            for step in range(steps):
                out = body(step, out)
            return out
        return lax.fori_loop(0, steps, body, out)

    def apply(v, high, low):
        both = jnp.dot(v, high, preferred_element_type=jnp.float32)
        return both[:rhs] + both[rhs:] + jnp.dot(v, low, preferred_element_type=jnp.float32)[:rhs]

    def hand_out(columns, partial, ref, group):
        for i, k in enumerate(columns):
            ref[nc + k] = partial[:, i * lanes : (i + 1) * lanes]
            if k:
                group.start(k, k + 1)

    def across(read):
        return lambda step: jnp.concatenate([read(step * pair + k) for k in range(pair)], axis=1)

    z_of = across(lambda k: plane[k, 0:feats, :])
    t_of = across(lambda k: plane[k, feats : feats + rhs, :])
    left = cached(lambda step: factors(z_of(step), True).T.astype(jnp.bfloat16))
    first_v = cached(lambda step: two(t_of(step)))

    to_line.arrived()
    rights = [
        factors(jnp.concatenate([line[k, 0:feats, :] for k in columns], axis=1), False).astype(jnp.bfloat16)
        for columns in order
    ]
    to_plane.arrived()

    for i, columns in enumerate(order):

        def first(step, out):
            tile = jnp.exp2(jnp.dot(left(step), rights[i], preferred_element_type=jnp.float32))
            high = tile.astype(jnp.bfloat16)
            low = (tile - high.astype(jnp.float32)).astype(jnp.bfloat16)
            khi[i, step] = high
            klo[i, step] = low
            return out + apply(first_v(step), high, low)

        hand_out(columns, total(first), part, give)

    noise = column(noise_ref, rhs, lanes)
    target = plane[0, feats : feats + rhs, :]
    image = part[nc] + noise * target
    give.arrived()
    for k in range(1, nc):
        image = image + part[k]

    wplane[0] = image
    wline[0] = image
    w_plane.start()
    w_line.start()
    tiny[0] = lane_sums([target * target, target * image, image * image])
    scalars.start()
    w_line.arrived()
    w_plane.arrived()
    scalars.arrived()

    sums = to_column(jnp.sum(tiny[...], axis=0))
    tt, tw, ww = sums[:rhs], sums[rhs : 2 * rhs], sums[2 * rhs : 3 * rhs]
    alpha = tt / tw
    beta = alpha * alpha * ww / tt - 1.0

    def direct(t, w):
        return (t - alpha * w) + beta * t

    d_of = across(lambda k: direct(plane[k, feats : feats + rhs, :], wplane[k]))
    second_v = cached(lambda step: two(d_of(step)))
    residual = target - alpha * image
    direction = direct(target, image)
    curved = noise * direction * direction
    for i, columns in enumerate(order):
        partial = total(lambda step, out: out + apply(second_v(step), khi[i, step], klo[i, step]))
        hand_out(columns, partial, part2, give2)
        for k in columns:
            curved = curved + direct(line[k, feats : feats + rhs, :], wline[k]) * part2[nc + k]
    tiny2[0] = lane_sums([curved, residual * residual])
    scalars2.start()
    image2 = part2[nc] + noise * direction
    give2.arrived()
    for k in range(1, nc):
        image2 = image2 + part2[k]
    scalars2.arrived()
    sums = to_column(jnp.sum(tiny2[...], axis=0))
    alpha2 = sums[rhs : 2 * rhs] / sums[:rhs]
    solution_ref[...] = alpha * target + alpha2 * direction
    residual_ref[...] = residual - alpha2 * image2
    for g in (to_line, to_plane, give, w_line, w_plane, scalars, give2, scalars2):
        g.sent()


def solution(mesh):
    nr, nc = mesh.shape["row"], mesh.shape["col"]

    def on_device(points, inverse_scale, targets, noise_var):
        feats, lanes = points.shape
        rhs = targets.shape[0]
        pair = 2 if nr % 2 == 0 else 1
        wide = 2 if nc % 2 == 0 else 1
        every = nr * nc
        f32 = jnp.float32
        block = jax.ShapeDtypeStruct((rhs, lanes), f32)
        dma = pltpu.SemaphoreType.DMA
        tiles = (nc // wide, nr // pair, pair * lanes, wide * lanes)
        anywhere = pl.BlockSpec(memory_space=pl.ANY)
        return pl.pallas_call(
            functools.partial(kernel, nr, nc, feats, rhs, lanes),
            out_shape=(pltpu.VMEM((rhs, lanes), f32),) * 2,
            in_specs=[anywhere] * 4,
            out_specs=(pl.BlockSpec(memory_space=pltpu.VMEM),) * 2,
            scratch_shapes=[
                pltpu.VMEM((feats, lanes), f32),
                pltpu.SMEM((feats,), f32),
                pltpu.SMEM((rhs,), f32),
                pltpu.VMEM((nr, feats + rhs, lanes), f32),
                pltpu.VMEM((nc, feats + rhs, lanes), f32),
                pltpu.VMEM((2 * nc, rhs, lanes), f32),
                pltpu.VMEM((nr, rhs, lanes), f32),
                pltpu.VMEM((nc, rhs, lanes), f32),
                pltpu.VMEM((2 * nc, rhs, lanes), f32),
                pltpu.VMEM((every, 1, lanes), f32),
                pltpu.VMEM((every, 1, lanes), f32),
                pltpu.VMEM(tiles, jnp.bfloat16),
                pltpu.VMEM(tiles, jnp.bfloat16),
                dma((5,)),
                dma((8,)),
                dma((8,)),
            ],
            compiler_params=pltpu.CompilerParams(
                collective_id=0, has_side_effects=True, vmem_limit_bytes=56 * 1024 * 1024
            ),
        )(points, inverse_scale, targets, noise_var)

    spec = P(None, ("row", "col"))
    return jax.shard_map(
        on_device, mesh=mesh, in_specs=(spec, P(), spec, P()), out_specs=(spec, spec), check_vma=False
    )
```

time: 30 us -> 26.8 us (0.89)
  Pallas kernels: 27.2 us -> 24.8 us
  local copies, waits for them, and re-layouts: 1.9 us -> 1.2 us
    pallas_call x1, Pallas kernels: 27.2 us -> 24.8 us  [on_device(): pl.pallas_call(functools.partial(kernel, nr, nc, feats, rhs, lanes), out_...]
    unnamed x4 -> x2, local copies, waits for them, and re-layouts: 1.9 us -> 1.2 us
where the time goes in v2:
time: 26.8 us; the launch traced here: 26.6 us
  Pallas kernels  24.8 us (93%)
  local copies, waits for them, and re-layouts  1.2 us (4%)
  between operations  0.64 us (2%)
    pallas_call x1, Pallas kernels, on_device(): pl.pallas_call(functools.partial(kernel, nr, nc, feats, rhs, lanes), out_...  24.8 us
    unnamed x2, local copies, waits for them, and re-layouts  1.2 us

profile of v2, /device:TPU:0, one launch (start us, length us, event | category | flops | bytes accessed | tf_op | source)
XLA Modules:
  0.0 26.6 jit_solution(9373240377464467328)
XLA Ops:
  0.6 24.8 %shard_map.59 = (f32[16,128]{1,0:T(8,128)S(1)}, f32[16,128]{1,0:T(8,128)S(1)}) custom-call(f32[8,128]{1,0:T(8,128)} %points_ref.1, f32[8]{0:T(128)} %scale_in.1, f32[16,128]{1,0:T(8,128)} %targets_ref.1, f32[16]{0:T(128)} %noise_in.1), custom_call_target="tpu_custom_call" | custom-call | tf_op jit(solution)/shard_map/pallas_call | solution.py:277
  25.4 0.6 %copy.8 = f32[16,128]{1,0:T(8,128)} copy(f32[16,128]{1,0:T(8,128)S(1)} %get-tuple-element.2) | data formatting | bytes 16384
  26.0 0.6 %copy.9 = f32[16,128]{1,0:T(8,128)} copy(f32[16,128]{1,0:T(8,128)S(1)} %get-tuple-element.3) | data formatting | bytes 16384

commit v3 on v2

--- a/solution.py
+++ b/solution.py
@@ -77,8 +77,17 @@
     r, c = lax.axis_index("row"), lax.axis_index("col")
     every = nr * nc
 
+    def turn(position, k, count):
+        moved = position + k
+        return jnp.where(moved >= count, moved - count, moved)
+
+    rows = [r] + [turn(r, k, nr) for k in range(1, nr)] if every <= 32 else None
+    cols = [c] + [turn(c, k, nc) for k in range(1, nc)] if every <= 32 else None
+
     def at(kr, kc):
-        return (lax.rem(r + kr, nr), lax.rem(c + kc, nc))
+        if rows is not None:
+            return (rows[kr], cols[kc])
+        return (turn(r, kr, nr), turn(c, kc, nc))
 
     barrier = pltpu.get_barrier_semaphore()
     loop(1, nr, lambda k: pl.semaphore_signal(barrier, inc=1, device_id=at(k, 0), device_id_type=MESH))
@@ -133,7 +142,7 @@
     along_col = lambda k: at(0, k)
     along_row = lambda k: at(k, 0)
     back_col = lambda k: at(0, nc - k)
-    anywhere = lambda k: at(k // nc, lax.rem(k, nc))
+    anywhere = lambda k: at(k // nc, k % nc)
     to_line = Group(line, nc, along_col)
     to_plane = Group(plane, nr, along_row)
     give = Group(part, nc, back_col, lambda k: nc + k)
@@ -220,10 +229,9 @@
     wplane[0] = image
     wline[0] = image
     w_plane.start()
-    w_line.start()
     tiny[0] = lane_sums([target * target, target * image, image * image])
     scalars.start()
-    w_line.arrived()
+    w_line.start()
     w_plane.arrived()
     scalars.arrived()
 
@@ -243,6 +251,8 @@
     for i, columns in enumerate(order):
         partial = total(lambda step, out: out + apply(second_v(step), khi[i, step], klo[i, step]))
         hand_out(columns, partial, part2, give2)
+        if i == 0:
+            w_line.arrived()
         for k in columns:
             curved = curved + direct(line[k, feats : feats + rhs, :], wline[k]) * part2[nc + k]
     tiny2[0] = lane_sums([curved, residual * residual])
@@ -260,6 +270,15 @@
         g.sent()
 
 
+def write(solution_ref, residual_ref, solution_out, residual_out, sem):
+    first = pltpu.make_async_copy(solution_ref, solution_out, sem.at[0])
+    second = pltpu.make_async_copy(residual_ref, residual_out, sem.at[1])
+    first.start()
+    second.start()
+    first.wait()
+    second.wait()
+
+
 def solution(mesh):
     nr, nc = mesh.shape["row"], mesh.shape["col"]
 
@@ -274,7 +293,7 @@
         dma = pltpu.SemaphoreType.DMA
         tiles = (nc // wide, nr // pair, pair * lanes, wide * lanes)
         anywhere = pl.BlockSpec(memory_space=pl.ANY)
-        return pl.pallas_call(
+        results = pl.pallas_call(
             functools.partial(kernel, nr, nc, feats, rhs, lanes),
             out_shape=(pltpu.VMEM((rhs, lanes), f32),) * 2,
             in_specs=[anywhere] * 4,
@@ -301,6 +320,13 @@
                 collective_id=0, has_side_effects=True, vmem_limit_bytes=56 * 1024 * 1024
             ),
         )(points, inverse_scale, targets, noise_var)
+        return pl.pallas_call(
+            write,
+            out_shape=(block, block),
+            in_specs=[pl.BlockSpec(memory_space=pltpu.VMEM)] * 2,
+            out_specs=(anywhere, anywhere),
+            scratch_shapes=[dma((2,))],
+        )(*results)
 
     spec = P(None, ("row", "col"))
     return jax.shard_map(

time: 26.8 us -> 28.2 us (1.052)
  Pallas kernels: 24.8 us -> 26.2 us
    pallas_call x0 -> x1, Pallas kernels: none -> 1.33 us  [on_device(): pl.pallas_call(write, out_shape=(block, block), in_specs=[pl.BlockSpec(me...]
    unnamed x2 -> x4, local copies, waits for them, and re-layouts: 1.2 us -> 1.18 us
where the time goes in v3:
time: 28.2 us; the launch traced here: 28 us
  Pallas kernels  26.2 us (93%)
  local copies, waits for them, and re-layouts  1.18 us (4%)
  between operations  0.65 us (2%)
    pallas_call x1, Pallas kernels, on_device(): pl.pallas_call(functools.partial(kernel, nr, nc, feats, rhs, lanes), out_...  24.9 us
    pallas_call x1, Pallas kernels, on_device(): pl.pallas_call(write, out_shape=(block, block), in_specs=[pl.BlockSpec(me...  1.33 us
    unnamed x4, local copies, waits for them, and re-layouts  1.18 us

profile of v3, /device:TPU:0, one launch (start us, length us, event | category | flops | bytes accessed | tf_op | source)
XLA Modules:
  0.0 28.0 jit_solution(3759818348740741252)
XLA Ops:
  0.6 24.9 %shard_map.59 = (f32[16,128]{1,0:T(8,128)S(1)}, f32[16,128]{1,0:T(8,128)S(1)}) custom-call(f32[8,128]{1,0:T(8,128)} %points_ref.1, f32[8]{0:T(128)} %scale_in.1, f32[16,128]{1,0:T(8,128)} %targets_ref.1, f32[16]{0:T(128)} %noise_in.1), custom_call_target="tpu_custom_call" | custom-call | tf_op jit(solution)/shard_map/pallas_call | solution.py:296
  25.5 0.0 copy-start
  25.5 0.6 %copy-done = f32[16,128]{1,0:T(8,128)} copy-done((f32[16,128]{1,0:T(8,128)}, f32[16,128]{1,0:T(8,128)S(1)}, u32[]{:S(2)}) %copy-start) | copy-done | bytes 8216
  26.1 0.0 copy-start.1
  26.1 0.6 %copy-done.1 = f32[16,128]{1,0:T(8,128)} copy-done((f32[16,128]{1,0:T(8,128)}, f32[16,128]{1,0:T(8,128)S(1)}, u32[]{:S(2)}) %copy-start.1) | copy-done | bytes 8216
  26.7 1.3 %shard_map.60 = (f32[16,128]{1,0:T(8,128)}, f32[16,128]{1,0:T(8,128)}) custom-call(f32[16,128]{1,0:T(8,128)} %copy-done, f32[16,128]{1,0:T(8,128)} %copy-done.1), custom_call_target="tpu_custom_call" | custom-call | tf_op jit(solution)/shard_map/pallas_call | solution.py:323
Async XLA Ops:
  25.5 0.6 %copy-start = (f32[16,128]{1,0:T(8,128)}, f32[16,128]{1,0:T(8,128)S(1)}, u32[]{:S(2)}) copy-start(f32[16,128]{1,0:T(8,128)S(1)} %get-tuple-element.4.solution_ref) | copy-start | bytes 24580
  26.1 0.6 %copy-start.1 = (f32[16,128]{1,0:T(8,128)}, f32[16,128]{1,0:T(8,128)S(1)}, u32[]{:S(2)}) copy-start(f32[16,128]{1,0:T(8,128)S(1)} %get-tuple-element.5.residual_ref) | copy-start | bytes 24580

commit v4 on v3

--- a/solution.py
+++ b/solution.py
@@ -7,6 +7,7 @@
 from jax.experimental.pallas import tpu as pltpu
 from jax.sharding import PartitionSpec as P
 
+FEW = 8
 MESH = pl.DeviceIdType.MESH
 ROOT = math.sqrt(1.0 / math.log(2.0))
 
@@ -70,8 +71,8 @@
 def kernel(
     nr, nc, feats, rhs, lanes,
     points_ref, scale_in, targets_ref, noise_in,
-    solution_ref, residual_ref,
-    raw, scale_ref, noise_ref, plane, line, part, wplane, wline, part2, tiny, tiny2, khi, klo,
+    base_ref, step_ref, along_ref, kept_ref, image_ref,
+    raw, scale_ref, noise_ref, zplane, zline, tplane, tline, part, wplane, wline, part2, tiny, tiny2, khi, klo, held,
     load_sem, send_sem, recv_sem,
 ):
     r, c = lax.axis_index("row"), lax.axis_index("col")
@@ -92,12 +93,11 @@
     barrier = pltpu.get_barrier_semaphore()
     loop(1, nr, lambda k: pl.semaphore_signal(barrier, inc=1, device_id=at(k, 0), device_id_type=MESH))
     loop(1, nc, lambda k: pl.semaphore_signal(barrier, inc=1, device_id=at(0, k), device_id_type=MESH))
-    own = pl.ds(feats, rhs)
     loads = [
         pltpu.make_async_copy(src, dst, load_sem.at[i])
         for i, (src, dst) in enumerate([
-            (points_ref, raw), (scale_in, scale_ref), (targets_ref, plane.at[0, own]),
-            (targets_ref, line.at[0, own]), (noise_in, noise_ref),
+            (points_ref, raw), (scale_in, scale_ref), (targets_ref, tplane.at[0]),
+            (targets_ref, tline.at[0]), (noise_in, noise_ref),
         ])
     ]
     for load in loads:
@@ -105,8 +105,8 @@
     loads[0].wait()
     loads[1].wait()
     scaled = raw[...] * column(scale_ref, feats, lanes)
-    plane[0, 0:feats, :] = scaled
-    line[0, 0:feats, :] = scaled
+    zplane[0] = scaled
+    zline[0] = scaled
     for load in loads[2:]:
         load.wait()
     pl.semaphore_wait(barrier, nr + nc - 2)
@@ -143,8 +143,10 @@
     along_row = lambda k: at(k, 0)
     back_col = lambda k: at(0, nc - k)
     anywhere = lambda k: at(k // nc, k % nc)
-    to_line = Group(line, nc, along_col)
-    to_plane = Group(plane, nr, along_row)
+    z_line = Group(zline, nc, along_col)
+    z_plane = Group(zplane, nr, along_row)
+    t_line = Group(tline, nc, along_col)
+    t_plane = Group(tplane, nr, along_row)
     give = Group(part, nc, back_col, lambda k: nc + k)
     w_line = Group(wline, nc, along_col)
     w_plane = Group(wplane, nr, along_row)
@@ -152,15 +154,17 @@
     give2 = Group(part2, nc, back_col, lambda k: nc + k)
     scalars2 = Group(tiny2, every, anywhere)
 
-    to_line.start()
-    to_plane.start()
+    z_line.start()
+    z_plane.start()
+    t_plane.start()
+    t_line.start()
 
     pair = 2 if nr % 2 == 0 else 1
     steps = nr // pair
     wide = 2 if nc % 2 == 0 else 1
     order = list(range(1, nc)) + [0]
     order = [order[i : i + wide] for i in range(0, nc, wide)]
-    few = steps <= 8
+    few = steps <= FEW
 
     def cached(make):
         held = {}
@@ -195,32 +199,53 @@
     def across(read):
         return lambda step: jnp.concatenate([read(step * pair + k) for k in range(pair)], axis=1)
 
-    z_of = across(lambda k: plane[k, 0:feats, :])
-    t_of = across(lambda k: plane[k, feats : feats + rhs, :])
+    z_of = across(lambda k: zplane[k])
+    t_of = across(lambda k: tplane[k])
     left = cached(lambda step: factors(z_of(step), True).T.astype(jnp.bfloat16))
     first_v = cached(lambda step: two(t_of(step)))
 
-    to_line.arrived()
+    z_line.arrived()
     rights = [
-        factors(jnp.concatenate([line[k, 0:feats, :] for k in columns], axis=1), False).astype(jnp.bfloat16)
+        factors(jnp.concatenate([zline[k] for k in columns], axis=1), False).astype(jnp.bfloat16)
         for columns in order
     ]
-    to_plane.arrived()
+    z_plane.arrived()
+
+    def low_part(tile):
+        return (tile - tile.astype(jnp.bfloat16).astype(jnp.float32)).astype(jnp.bfloat16)
+
+    def make_tile(i, step):
+        tile = jnp.exp2(jnp.dot(left(step), rights[i], preferred_element_type=jnp.float32))
+        high = tile.astype(jnp.bfloat16)
+        khi[i, step] = high
+        if few:
+            held[i, step] = tile
+        else:
+            klo[i, step] = low_part(tile)
+        return high
+
+    def first(i, step, out, high):
+        both = jnp.dot(first_v(step), high, preferred_element_type=jnp.float32)
+        return out + both[:rhs] + both[rhs:]
 
     for i, columns in enumerate(order):
-
-        def first(step, out):
-            tile = jnp.exp2(jnp.dot(left(step), rights[i], preferred_element_type=jnp.float32))
-            high = tile.astype(jnp.bfloat16)
-            low = (tile - high.astype(jnp.float32)).astype(jnp.bfloat16)
-            khi[i, step] = high
-            klo[i, step] = low
-            return out + apply(first_v(step), high, low)
-
-        hand_out(columns, total(first), part, give)
+        if few and i == 0:
+            for step in range(steps):
+                make_tile(i, step)
+            t_plane.arrived()
+            partial = total(lambda step, out: first(i, step, out, khi[i, step]))
+        else:
+            if i == 0:
+                t_plane.arrived()
+            partial = total(lambda step, out: first(i, step, out, make_tile(i, step)))
+        hand_out(columns, partial, part, give)
+    if few:
+        for i in range(len(order)):
+            for step in range(steps):
+                klo[i, step] = low_part(held[i, step])
 
     noise = column(noise_ref, rhs, lanes)
-    target = plane[0, feats : feats + rhs, :]
+    target = tplane[0]
     image = part[nc] + noise * target
     give.arrived()
     for k in range(1, nc):
@@ -243,7 +268,7 @@
     def direct(t, w):
         return (t - alpha * w) + beta * t
 
-    d_of = across(lambda k: direct(plane[k, feats : feats + rhs, :], wplane[k]))
+    d_of = across(lambda k: direct(tplane[k], wplane[k]))
     second_v = cached(lambda step: two(d_of(step)))
     residual = target - alpha * image
     direction = direct(target, image)
@@ -253,30 +278,25 @@
         hand_out(columns, partial, part2, give2)
         if i == 0:
             w_line.arrived()
+            t_line.arrived()
         for k in columns:
-            curved = curved + direct(line[k, feats : feats + rhs, :], wline[k]) * part2[nc + k]
+            curved = curved + direct(tline[k], wline[k]) * part2[nc + k]
     tiny2[0] = lane_sums([curved, residual * residual])
     scalars2.start()
+    base_ref[...] = alpha * target
+    along_ref[...] = direction
+    kept_ref[...] = residual
     image2 = part2[nc] + noise * direction
     give2.arrived()
     for k in range(1, nc):
         image2 = image2 + part2[k]
+    image_ref[...] = image2
     scalars2.arrived()
     sums = to_column(jnp.sum(tiny2[...], axis=0))
     alpha2 = sums[rhs : 2 * rhs] / sums[:rhs]
-    solution_ref[...] = alpha * target + alpha2 * direction
-    residual_ref[...] = residual - alpha2 * image2
-    for g in (to_line, to_plane, give, w_line, w_plane, scalars, give2, scalars2):
+    step_ref[...] = jnp.broadcast_to(alpha2, (rhs, lanes))
+    for g in (z_line, z_plane, t_plane, t_line, give, w_line, w_plane, scalars, give2, scalars2):
         g.sent()
-
-
-def write(solution_ref, residual_ref, solution_out, residual_out, sem):
-    first = pltpu.make_async_copy(solution_ref, solution_out, sem.at[0])
-    second = pltpu.make_async_copy(residual_ref, residual_out, sem.at[1])
-    first.start()
-    second.start()
-    first.wait()
-    second.wait()
 
 
 def solution(mesh):
@@ -289,21 +309,22 @@
         wide = 2 if nc % 2 == 0 else 1
         every = nr * nc
         f32 = jnp.float32
-        block = jax.ShapeDtypeStruct((rhs, lanes), f32)
         dma = pltpu.SemaphoreType.DMA
         tiles = (nc // wide, nr // pair, pair * lanes, wide * lanes)
         anywhere = pl.BlockSpec(memory_space=pl.ANY)
-        results = pl.pallas_call(
+        base, step, along, kept, image = pl.pallas_call(
             functools.partial(kernel, nr, nc, feats, rhs, lanes),
-            out_shape=(pltpu.VMEM((rhs, lanes), f32),) * 2,
+            out_shape=(pltpu.VMEM((rhs, lanes), f32),) * 5,
             in_specs=[anywhere] * 4,
-            out_specs=(pl.BlockSpec(memory_space=pltpu.VMEM),) * 2,
+            out_specs=(pl.BlockSpec(memory_space=pltpu.VMEM),) * 5,
             scratch_shapes=[
                 pltpu.VMEM((feats, lanes), f32),
                 pltpu.SMEM((feats,), f32),
                 pltpu.SMEM((rhs,), f32),
-                pltpu.VMEM((nr, feats + rhs, lanes), f32),
-                pltpu.VMEM((nc, feats + rhs, lanes), f32),
+                pltpu.VMEM((nr, feats, lanes), f32),
+                pltpu.VMEM((nc, feats, lanes), f32),
+                pltpu.VMEM((nr, rhs, lanes), f32),
+                pltpu.VMEM((nc, rhs, lanes), f32),
                 pltpu.VMEM((2 * nc, rhs, lanes), f32),
                 pltpu.VMEM((nr, rhs, lanes), f32),
                 pltpu.VMEM((nc, rhs, lanes), f32),
@@ -312,21 +333,16 @@
                 pltpu.VMEM((every, 1, lanes), f32),
                 pltpu.VMEM(tiles, jnp.bfloat16),
                 pltpu.VMEM(tiles, jnp.bfloat16),
+                pltpu.VMEM(tiles if nr // pair <= FEW else (8, 128), f32),
                 dma((5,)),
-                dma((8,)),
-                dma((8,)),
+                dma((10,)),
+                dma((10,)),
             ],
             compiler_params=pltpu.CompilerParams(
                 collective_id=0, has_side_effects=True, vmem_limit_bytes=56 * 1024 * 1024
             ),
         )(points, inverse_scale, targets, noise_var)
-        return pl.pallas_call(
-            write,
-            out_shape=(block, block),
-            in_specs=[pl.BlockSpec(memory_space=pltpu.VMEM)] * 2,
-            out_specs=(anywhere, anywhere),
-            scratch_shapes=[dma((2,))],
-        )(*results)
+        return base + step * along, kept - step * image
 
     spec = P(None, ("row", "col"))
     return jax.shard_map(

time: 28.2 us -> 25.2 us (0.89)
  Pallas kernels: 26.2 us -> 23.8 us
  local copies, waits for them, and re-layouts: 1.18 us -> 0 us
  other arithmetic: 0 us -> 0.61 us
    pallas_call x1 -> x0, Pallas kernels: 1.33 us -> none  [on_device(): pl.pallas_call(write, out_shape=(block, block), in_specs=[pl.BlockSpec(me...]
    unnamed x4 -> x0, local copies, waits for them, and re-layouts: 1.18 us -> none
    pallas_call x1, Pallas kernels: 24.9 us -> 23.8 us  [on_device(): pl.pallas_call(functools.partial(kernel, nr, nc, feats, rhs, lanes), out_...]
    sub x0 -> x1, other arithmetic: none -> 0.61 us  [on_device(): return (base + step * along, kept - step * image)]
where the time goes in v4:
time: 25.2 us; the launch traced here: 25 us
  Pallas kernels  23.8 us (94%)
  between operations  0.64 us (3%)
  other arithmetic  0.61 us (2%)
    pallas_call x1, Pallas kernels, on_device(): pl.pallas_call(functools.partial(kernel, nr, nc, feats, rhs, lanes), out_...  23.8 us
    sub x1, other arithmetic, on_device(): return (base + step * along, kept - step * image)  0.61 us

profile of v4, /device:TPU:0, one launch (start us, length us, event | category | flops | bytes accessed | tf_op | source)
XLA Modules:
  0.0 25.0 jit_solution(1769991085036032025)
XLA Ops:
  0.6 23.8 %shard_map.59 = (f32[16,128]{1,0:T(8,128)S(1)}, f32[16,128]{1,0:T(8,128)S(1)}, f32[16,128]{1,0:T(8,128)S(1)}, f32[16,128]{1,0:T(8,128)S(1)}, f32[16,128]{1,0:T(8,128)S(1)}) custom-call(f32[8,128]{1,0:T(8,128)} %points_ref.1, f32[8]{0:T(128)} %scale_in.1, f32[16,128]{1,0:T(8,128)} %targets_ref.1, f32[16]{0:T(128)} %noise_in.1), custom_call_target="tpu_custom_call" | custom-call | tf_op jit(solution)/shard_map/pallas_call | solution.py:315
  24.4 0.6 %multiply_subtract_fusion = (f32[16,128]{1,0:T(8,128)}, f32[16,128]{1,0:T(8,128)}) fusion(f32[16,128]{1,0:T(8,128)S(1)} %get-tuple-element.10, f32[16,128]{1,0:T(8,128)S(1)} %get-tuple-element.8, f32[16,128]{1,0:T(8,128)S(1)} %get-tuple-element.11, f32[16,128]{1,0:T(8,128)S(1)} %get-tuple-element.7, f32[16,128]{1,0:T(8,128)S(1)} %get-tuple-element.9), kind=kLoop, calls=%fused_computation | loop fusion | flops 8192 | bytes 57344 | tf_op jit(solution)/shard_map/sub | solution.py:345

commit v5 on v4

--- a/solution.py
+++ b/solution.py
@@ -72,7 +72,7 @@
     nr, nc, feats, rhs, lanes,
     points_ref, scale_in, targets_ref, noise_in,
     base_ref, step_ref, along_ref, kept_ref, image_ref,
-    raw, scale_ref, noise_ref, zplane, zline, tplane, tline, part, wplane, wline, part2, tiny, tiny2, khi, klo, held,
+    raw, scale_ref, noise_ref, zplane, zline, tplane, tline, part, wplane, wline, part2, early, tiny, khi, klo, held,
     load_sem, send_sem, recv_sem,
 ):
     r, c = lax.axis_index("row"), lax.axis_index("col")
@@ -150,9 +150,9 @@
     give = Group(part, nc, back_col, lambda k: nc + k)
     w_line = Group(wline, nc, along_col)
     w_plane = Group(wplane, nr, along_row)
-    scalars = Group(tiny, every, anywhere)
+    scalars = Group(early, nc, along_col)
     give2 = Group(part2, nc, back_col, lambda k: nc + k)
-    scalars2 = Group(tiny2, every, anywhere)
+    scalars2 = Group(tiny, every, anywhere)
 
     z_line.start()
     z_plane.start()
@@ -239,36 +239,46 @@
                 t_plane.arrived()
             partial = total(lambda step, out: first(i, step, out, make_tile(i, step)))
         hand_out(columns, partial, part, give)
+    target = tplane[0]
+    t_line.arrived()
+    along, squared = jnp.zeros((rhs, lanes), jnp.float32), jnp.zeros((rhs, lanes), jnp.float32)
+    for k in range(nc):
+        along = along + tline[k] * part[nc + k]
+        squared = squared + part[nc + k] * part[nc + k]
+    early[0] = lane_sums([along, squared, target * target])
+    scalars.start()
     if few:
         for i in range(len(order)):
             for step in range(steps):
                 klo[i, step] = low_part(held[i, step])
 
     noise = column(noise_ref, rhs, lanes)
-    target = tplane[0]
     image = part[nc] + noise * target
     give.arrived()
     for k in range(1, nc):
         image = image + part[k]
 
-    wplane[0] = image
+    scalars.arrived()
+    wplane[0, 0:rhs, :] = image
+    wplane[0, rhs : rhs + 8, :] = jnp.broadcast_to(jnp.sum(early[...], axis=0), (8, lanes))
     wline[0] = image
     w_plane.start()
-    tiny[0] = lane_sums([target * target, target * image, image * image])
-    scalars.start()
     w_line.start()
     w_plane.arrived()
-    scalars.arrived()
-
-    sums = to_column(jnp.sum(tiny[...], axis=0))
-    tt, tw, ww = sums[:rhs], sums[rhs : 2 * rhs], sums[2 * rhs : 3 * rhs]
+
+    row = wplane[0, rhs : rhs + 8, :]
+    for k in range(1, nr):
+        row = row + wplane[k, rhs : rhs + 8, :]
+    sums = to_column(row[0:1])
+    tkt, spread, tt = sums[:rhs], sums[rhs : 2 * rhs], sums[2 * rhs : 3 * rhs]
+    tw = tkt + noise * tt
     alpha = tt / tw
-    beta = alpha * alpha * ww / tt - 1.0
+    guess = alpha * alpha * (nc * spread + 2.0 * noise * tkt + noise * noise * tt) / tt - 1.0
 
     def direct(t, w):
-        return (t - alpha * w) + beta * t
-
-    d_of = across(lambda k: direct(tplane[k], wplane[k]))
+        return (t - alpha * w) + guess * t
+
+    d_of = across(lambda k: direct(tplane[k], wplane[k, 0:rhs, :]))
     second_v = cached(lambda step: two(d_of(step)))
     residual = target - alpha * image
     direction = direct(target, image)
@@ -278,23 +288,23 @@
         hand_out(columns, partial, part2, give2)
         if i == 0:
             w_line.arrived()
-            t_line.arrived()
         for k in columns:
             curved = curved + direct(tline[k], wline[k]) * part2[nc + k]
-    tiny2[0] = lane_sums([curved, residual * residual])
+    tiny[0] = lane_sums([curved, residual * residual, direction * image])
     scalars2.start()
     base_ref[...] = alpha * target
-    along_ref[...] = direction
     kept_ref[...] = residual
     image2 = part2[nc] + noise * direction
     give2.arrived()
     for k in range(1, nc):
         image2 = image2 + part2[k]
-    image_ref[...] = image2
     scalars2.arrived()
-    sums = to_column(jnp.sum(tiny2[...], axis=0))
-    alpha2 = sums[rhs : 2 * rhs] / sums[:rhs]
-    step_ref[...] = jnp.broadcast_to(alpha2, (rhs, lanes))
+    sums = to_column(jnp.sum(tiny[...], axis=0))
+    curvature, norm, mixed = sums[:rhs], sums[rhs : 2 * rhs], sums[2 * rhs : 3 * rhs]
+    missed = norm / tt - guess
+    step_ref[...] = norm / (curvature + 2.0 * missed * mixed + missed * missed * tw)
+    along_ref[...] = direction + missed * target
+    image_ref[...] = image2 + missed * image
     for g in (z_line, z_plane, t_plane, t_line, give, w_line, w_plane, scalars, give2, scalars2):
         g.sent()
 
@@ -326,10 +336,10 @@
                 pltpu.VMEM((nr, rhs, lanes), f32),
                 pltpu.VMEM((nc, rhs, lanes), f32),
                 pltpu.VMEM((2 * nc, rhs, lanes), f32),
-                pltpu.VMEM((nr, rhs, lanes), f32),
+                pltpu.VMEM((nr, rhs + 8, lanes), f32),
                 pltpu.VMEM((nc, rhs, lanes), f32),
                 pltpu.VMEM((2 * nc, rhs, lanes), f32),
-                pltpu.VMEM((every, 1, lanes), f32),
+                pltpu.VMEM((nc, 1, lanes), f32),
                 pltpu.VMEM((every, 1, lanes), f32),
                 pltpu.VMEM(tiles, jnp.bfloat16),
                 pltpu.VMEM(tiles, jnp.bfloat16),

time: 25.2 us -> 24.7 us (0.980)
  Pallas kernels: 23.8 us -> 23.3 us
    pallas_call x1, Pallas kernels: 23.8 us -> 23.3 us  [on_device(): pl.pallas_call(functools.partial(kernel, nr, nc, feats, rhs, lanes), out_...]
where the time goes in v5:
time: 24.7 us; the launch traced here: 24.5 us
  Pallas kernels  23.3 us (94%)
  between operations  0.64 us (3%)
  other arithmetic  0.61 us (2%)
    pallas_call x1, Pallas kernels, on_device(): pl.pallas_call(functools.partial(kernel, nr, nc, feats, rhs, lanes), out_...  23.3 us
    sub x1, other arithmetic, on_device(): return (base + step * along, kept - step * image)  0.61 us

profile of v5, /device:TPU:0, one launch (start us, length us, event | category | flops | bytes accessed | tf_op | source)
XLA Modules:
  0.0 24.5 jit_solution(1101653356219813957)
XLA Ops:
  0.6 23.3 %shard_map.59 = (f32[16,128]{1,0:T(8,128)S(1)}, f32[16,128]{1,0:T(8,128)S(1)}, f32[16,128]{1,0:T(8,128)S(1)}, f32[16,128]{1,0:T(8,128)S(1)}, f32[16,128]{1,0:T(8,128)S(1)}) custom-call(f32[8,128]{1,0:T(8,128)} %points_ref.1, f32[8]{0:T(128)} %scale_in.1, f32[16,128]{1,0:T(8,128)} %targets_ref.1, f32[16]{0:T(128)} %noise_in.1), custom_call_target="tpu_custom_call" | custom-call | tf_op jit(solution)/shard_map/pallas_call | solution.py:325
  23.9 0.6 %multiply_subtract_fusion = (f32[16,128]{1,0:T(8,128)}, f32[16,128]{1,0:T(8,128)}) fusion(f32[16,128]{1,0:T(8,128)S(1)} %get-tuple-element.10, f32[16,128]{1,0:T(8,128)S(1)} %get-tuple-element.8, f32[16,128]{1,0:T(8,128)S(1)} %get-tuple-element.11, f32[16,128]{1,0:T(8,128)S(1)} %get-tuple-element.7, f32[16,128]{1,0:T(8,128)S(1)} %get-tuple-element.9), kind=kLoop, calls=%fused_computation | loop fusion | flops 8192 | bytes 57344 | tf_op jit(solution)/shard_map/sub | solution.py:355

commit v6 on v5

--- a/solution.py
+++ b/solution.py
@@ -73,7 +73,7 @@
     points_ref, scale_in, targets_ref, noise_in,
     base_ref, step_ref, along_ref, kept_ref, image_ref,
     raw, scale_ref, noise_ref, zplane, zline, tplane, tline, part, wplane, wline, part2, early, tiny, khi, klo, held,
-    load_sem, send_sem, recv_sem,
+    load_sem, send_sem, recv_sem, line_sem,
 ):
     r, c = lax.axis_index("row"), lax.axis_index("col")
     every = nr * nc
@@ -114,16 +114,18 @@
     class Group:
         count = 0
 
-        def __init__(self, ref, last, peer, src=lambda k: 0):
+        def __init__(self, ref, last, peer, src=lambda k: 0, slot_sems=None):
             self.ref, self.last, self.peer, self.src = ref, last, peer, src
+            self.slot_sems = slot_sems
             self.sem = Group.count
             Group.count += 1
 
         def start(self, low=1, high=None):
             def one(k):
+                arrival = recv_sem.at[self.sem] if self.slot_sems is None else self.slot_sems.at[k]
                 pltpu.make_async_remote_copy(
                     src_ref=self.ref.at[self.src(k)], dst_ref=self.ref.at[k],
-                    send_sem=send_sem.at[self.sem], recv_sem=recv_sem.at[self.sem],
+                    send_sem=send_sem.at[self.sem], recv_sem=arrival,
                     device_id=self.peer(k), device_id_type=MESH,
                 ).start()
 
@@ -132,6 +134,9 @@
         def wait(self, sem):
             slots = self.ref.at[pl.ds(1, self.last - 1)]
             pltpu.make_async_copy(slots, slots, sem.at[self.sem]).wait()
+
+        def wait_slot(self, k):
+            pltpu.make_async_copy(self.ref.at[k], self.ref.at[k], self.slot_sems.at[k]).wait()
 
         def arrived(self):
             self.wait(recv_sem)
@@ -143,7 +148,7 @@
     along_row = lambda k: at(k, 0)
     back_col = lambda k: at(0, nc - k)
     anywhere = lambda k: at(k // nc, k % nc)
-    z_line = Group(zline, nc, along_col)
+    z_line = Group(zline, nc, along_col, slot_sems=line_sem)
     z_plane = Group(zplane, nr, along_row)
     t_line = Group(tline, nc, along_col)
     t_plane = Group(tplane, nr, along_row)
@@ -162,7 +167,7 @@
     pair = 2 if nr % 2 == 0 else 1
     steps = nr // pair
     wide = 2 if nc % 2 == 0 else 1
-    order = list(range(1, nc)) + [0]
+    order = sorted(range(1, nc), key=lambda k: min(k, nc - k)) + [0]
     order = [order[i : i + wide] for i in range(0, nc, wide)]
     few = steps <= FEW
 
@@ -178,8 +183,8 @@
 
         return get
 
-    def total(body):
-        out = jnp.zeros((rhs, wide * lanes), jnp.float32)
+    def total(body, width):
+        out = jnp.zeros((rhs, width * lanes), jnp.float32)
         if few:
             for step in range(steps):
                 out = body(step, out)
@@ -204,41 +209,39 @@
     left = cached(lambda step: factors(z_of(step), True).T.astype(jnp.bfloat16))
     first_v = cached(lambda step: two(t_of(step)))
 
-    z_line.arrived()
-    rights = [
-        factors(jnp.concatenate([zline[k] for k in columns], axis=1), False).astype(jnp.bfloat16)
-        for columns in order
-    ]
     z_plane.arrived()
 
     def low_part(tile):
         return (tile - tile.astype(jnp.bfloat16).astype(jnp.float32)).astype(jnp.bfloat16)
 
-    def make_tile(i, step):
-        tile = jnp.exp2(jnp.dot(left(step), rights[i], preferred_element_type=jnp.float32))
+    def make_tile(k, right, step):
+        tile = jnp.exp2(jnp.dot(left(step), right, preferred_element_type=jnp.float32))
         high = tile.astype(jnp.bfloat16)
-        khi[i, step] = high
+        khi[k, step] = high
         if few:
-            held[i, step] = tile
+            held[k, step] = tile
         else:
-            klo[i, step] = low_part(tile)
+            klo[k, step] = low_part(tile)
         return high
 
-    def first(i, step, out, high):
+    def first(step, out, high):
         both = jnp.dot(first_v(step), high, preferred_element_type=jnp.float32)
         return out + both[:rhs] + both[rhs:]
 
-    for i, columns in enumerate(order):
-        if few and i == 0:
+    for k in range(nc):
+        if k:
+            z_line.wait_slot(k)
+        right = factors(zline[k], False).astype(jnp.bfloat16)
+        if few and k == 0:
             for step in range(steps):
-                make_tile(i, step)
+                make_tile(k, right, step)
             t_plane.arrived()
-            partial = total(lambda step, out: first(i, step, out, khi[i, step]))
+            partial = total(lambda step, out: first(step, out, khi[k, step]), 1)
         else:
-            if i == 0:
+            if k == 0:
                 t_plane.arrived()
-            partial = total(lambda step, out: first(i, step, out, make_tile(i, step)))
-        hand_out(columns, partial, part, give)
+            partial = total(lambda step, out: first(step, out, make_tile(k, right, step)), 1)
+        hand_out([k], partial, part, give)
     target = tplane[0]
     t_line.arrived()
     along, squared = jnp.zeros((rhs, lanes), jnp.float32), jnp.zeros((rhs, lanes), jnp.float32)
@@ -248,9 +251,9 @@
     early[0] = lane_sums([along, squared, target * target])
     scalars.start()
     if few:
-        for i in range(len(order)):
+        for k in range(nc):
             for step in range(steps):
-                klo[i, step] = low_part(held[i, step])
+                klo[k, step] = low_part(held[k, step])
 
     noise = column(noise_ref, rhs, lanes)
     image = part[nc] + noise * target
@@ -284,7 +287,10 @@
     direction = direct(target, image)
     curved = noise * direction * direction
     for i, columns in enumerate(order):
-        partial = total(lambda step, out: out + apply(second_v(step), khi[i, step], klo[i, step]))
+        beside = lambda ref, step: jnp.concatenate([ref[k, step] for k in columns], axis=1)
+        partial = total(
+            lambda step, out: out + apply(second_v(step), beside(khi, step), beside(klo, step)), len(columns)
+        )
         hand_out(columns, partial, part2, give2)
         if i == 0:
             w_line.arrived()
@@ -316,11 +322,10 @@
         feats, lanes = points.shape
         rhs = targets.shape[0]
         pair = 2 if nr % 2 == 0 else 1
-        wide = 2 if nc % 2 == 0 else 1
         every = nr * nc
         f32 = jnp.float32
         dma = pltpu.SemaphoreType.DMA
-        tiles = (nc // wide, nr // pair, pair * lanes, wide * lanes)
+        tiles = (nc, nr // pair, pair * lanes, lanes)
         anywhere = pl.BlockSpec(memory_space=pl.ANY)
         base, step, along, kept, image = pl.pallas_call(
             functools.partial(kernel, nr, nc, feats, rhs, lanes),
@@ -347,6 +352,7 @@
                 dma((5,)),
                 dma((10,)),
                 dma((10,)),
+                dma((nc,)),
             ],
             compiler_params=pltpu.CompilerParams(
                 collective_id=0, has_side_effects=True, vmem_limit_bytes=56 * 1024 * 1024

time: 24.7 us -> 26.2 us (1.061)
  Pallas kernels: 23.3 us -> 24.7 us
    pallas_call x1, Pallas kernels: 23.3 us -> 24.7 us  [on_device(): pl.pallas_call(functools.partial(kernel, nr, nc, feats, rhs, lanes), out_...]
where the time goes in v6:
time: 26.2 us; the launch traced here: 26 us
  Pallas kernels  24.7 us (94%)
  between operations  0.64 us (2%)
  other arithmetic  0.61 us (2%)
    pallas_call x1, Pallas kernels, on_device(): pl.pallas_call(functools.partial(kernel, nr, nc, feats, rhs, lanes), out_...  24.7 us
    sub x1, other arithmetic, on_device(): return (base + step * along, kept - step * image)  0.61 us

profile of v6, /device:TPU:0, one launch (start us, length us, event | category | flops | bytes accessed | tf_op | source)
XLA Modules:
  0.0 26.0 jit_solution(6400877048925262159)
XLA Ops:
  0.6 24.7 %shard_map.59 = (f32[16,128]{1,0:T(8,128)S(1)}, f32[16,128]{1,0:T(8,128)S(1)}, f32[16,128]{1,0:T(8,128)S(1)}, f32[16,128]{1,0:T(8,128)S(1)}, f32[16,128]{1,0:T(8,128)S(1)}) custom-call(f32[8,128]{1,0:T(8,128)} %points_ref.1, f32[8]{0:T(128)} %scale_in.1, f32[16,128]{1,0:T(8,128)} %targets_ref.1, f32[16]{0:T(128)} %noise_in.1), custom_call_target="tpu_custom_call" | custom-call | tf_op jit(solution)/shard_map/pallas_call | solution.py:330
  25.4 0.6 %multiply_subtract_fusion = (f32[16,128]{1,0:T(8,128)}, f32[16,128]{1,0:T(8,128)}) fusion(f32[16,128]{1,0:T(8,128)S(1)} %get-tuple-element.10, f32[16,128]{1,0:T(8,128)S(1)} %get-tuple-element.8, f32[16,128]{1,0:T(8,128)S(1)} %get-tuple-element.11, f32[16,128]{1,0:T(8,128)S(1)} %get-tuple-element.7, f32[16,128]{1,0:T(8,128)S(1)} %get-tuple-element.9), kind=kLoop, calls=%fused_computation | loop fusion | flops 8192 | bytes 57344 | tf_op jit(solution)/shard_map/sub | solution.py:361

commit v7 on v5

--- a/solution.py
+++ b/solution.py
@@ -73,7 +73,7 @@
     points_ref, scale_in, targets_ref, noise_in,
     base_ref, step_ref, along_ref, kept_ref, image_ref,
     raw, scale_ref, noise_ref, zplane, zline, tplane, tline, part, wplane, wline, part2, early, tiny, khi, klo, held,
-    load_sem, send_sem, recv_sem,
+    load_sem, send_sem, recv_sem, line_sem,
 ):
     r, c = lax.axis_index("row"), lax.axis_index("col")
     every = nr * nc
@@ -114,16 +114,18 @@
     class Group:
         count = 0
 
-        def __init__(self, ref, last, peer, src=lambda k: 0):
+        def __init__(self, ref, last, peer, src=lambda k: 0, slot_sems=None):
             self.ref, self.last, self.peer, self.src = ref, last, peer, src
+            self.slot_sems = slot_sems
             self.sem = Group.count
             Group.count += 1
 
         def start(self, low=1, high=None):
             def one(k):
+                arrival = recv_sem.at[self.sem] if self.slot_sems is None else self.slot_sems.at[k]
                 pltpu.make_async_remote_copy(
                     src_ref=self.ref.at[self.src(k)], dst_ref=self.ref.at[k],
-                    send_sem=send_sem.at[self.sem], recv_sem=recv_sem.at[self.sem],
+                    send_sem=send_sem.at[self.sem], recv_sem=arrival,
                     device_id=self.peer(k), device_id_type=MESH,
                 ).start()
 
@@ -133,24 +135,36 @@
             slots = self.ref.at[pl.ds(1, self.last - 1)]
             pltpu.make_async_copy(slots, slots, sem.at[self.sem]).wait()
 
+        def wait_slot(self, k):
+            pltpu.make_async_copy(self.ref.at[k], self.ref.at[k], self.slot_sems.at[k]).wait()
+
         def arrived(self):
             self.wait(recv_sem)
 
         def sent(self):
             self.wait(send_sem)
 
-    along_col = lambda k: at(0, k)
+    def across_col(k):
+        other, bit = c, 1
+        while bit < nc:
+            if k & bit:
+                other = other + bit * (1 - 2 * lax.rem(lax.div(c, bit), 2))
+            bit *= 2
+        return (r, other)
+
+    paired = nc & (nc - 1) == 0
+    along_col = across_col if paired else lambda k: at(0, k)
     along_row = lambda k: at(k, 0)
-    back_col = lambda k: at(0, nc - k)
+    back_col = across_col if paired else lambda k: at(0, nc - k)
     anywhere = lambda k: at(k // nc, k % nc)
-    z_line = Group(zline, nc, along_col)
+    z_line = Group(zline, nc, along_col, slot_sems=line_sem)
     z_plane = Group(zplane, nr, along_row)
     t_line = Group(tline, nc, along_col)
     t_plane = Group(tplane, nr, along_row)
     give = Group(part, nc, back_col, lambda k: nc + k)
     w_line = Group(wline, nc, along_col)
     w_plane = Group(wplane, nr, along_row)
-    scalars = Group(early, nc, along_col)
+    scalars = Group(early, every, anywhere)
     give2 = Group(part2, nc, back_col, lambda k: nc + k)
     scalars2 = Group(tiny, every, anywhere)
 
@@ -162,8 +176,7 @@
     pair = 2 if nr % 2 == 0 else 1
     steps = nr // pair
     wide = 2 if nc % 2 == 0 else 1
-    order = list(range(1, nc)) + [0]
-    order = [order[i : i + wide] for i in range(0, nc, wide)]
+    order = [list(range(i, i + wide)) for i in range(0, nc, wide)]
     few = steps <= FEW
 
     def cached(make):
@@ -204,18 +217,13 @@
     left = cached(lambda step: factors(z_of(step), True).T.astype(jnp.bfloat16))
     first_v = cached(lambda step: two(t_of(step)))
 
-    z_line.arrived()
-    rights = [
-        factors(jnp.concatenate([zline[k] for k in columns], axis=1), False).astype(jnp.bfloat16)
-        for columns in order
-    ]
     z_plane.arrived()
 
     def low_part(tile):
         return (tile - tile.astype(jnp.bfloat16).astype(jnp.float32)).astype(jnp.bfloat16)
 
-    def make_tile(i, step):
-        tile = jnp.exp2(jnp.dot(left(step), rights[i], preferred_element_type=jnp.float32))
+    def make_tile(i, right, step):
+        tile = jnp.exp2(jnp.dot(left(step), right, preferred_element_type=jnp.float32))
         high = tile.astype(jnp.bfloat16)
         khi[i, step] = high
         if few:
@@ -229,15 +237,19 @@
         return out + both[:rhs] + both[rhs:]
 
     for i, columns in enumerate(order):
+        for k in columns:
+            if k:
+                z_line.wait_slot(k)
+        right = factors(jnp.concatenate([zline[k] for k in columns], axis=1), False).astype(jnp.bfloat16)
         if few and i == 0:
             for step in range(steps):
-                make_tile(i, step)
+                make_tile(i, right, step)
             t_plane.arrived()
             partial = total(lambda step, out: first(i, step, out, khi[i, step]))
         else:
             if i == 0:
                 t_plane.arrived()
-            partial = total(lambda step, out: first(i, step, out, make_tile(i, step)))
+            partial = total(lambda step, out: first(i, step, out, make_tile(i, right, step)))
         hand_out(columns, partial, part, give)
     target = tplane[0]
     t_line.arrived()
@@ -258,35 +270,31 @@
     for k in range(1, nc):
         image = image + part[k]
 
-    scalars.arrived()
-    wplane[0, 0:rhs, :] = image
-    wplane[0, rhs : rhs + 8, :] = jnp.broadcast_to(jnp.sum(early[...], axis=0), (8, lanes))
+    wplane[0] = image
     wline[0] = image
     w_plane.start()
     w_line.start()
-    w_plane.arrived()
-
-    row = wplane[0, rhs : rhs + 8, :]
-    for k in range(1, nr):
-        row = row + wplane[k, rhs : rhs + 8, :]
-    sums = to_column(row[0:1])
+    scalars.arrived()
+    sums = to_column(jnp.sum(early[...], axis=0))
     tkt, spread, tt = sums[:rhs], sums[rhs : 2 * rhs], sums[2 * rhs : 3 * rhs]
     tw = tkt + noise * tt
     alpha = tt / tw
     guess = alpha * alpha * (nc * spread + 2.0 * noise * tkt + noise * noise * tt) / tt - 1.0
 
+    w_plane.arrived()
+
     def direct(t, w):
         return (t - alpha * w) + guess * t
 
-    d_of = across(lambda k: direct(tplane[k], wplane[k, 0:rhs, :]))
+    d_of = across(lambda k: direct(tplane[k], wplane[k]))
     second_v = cached(lambda step: two(d_of(step)))
     residual = target - alpha * image
     direction = direct(target, image)
     curved = noise * direction * direction
-    for i, columns in enumerate(order):
+    for i, columns in reversed(list(enumerate(order))):
         partial = total(lambda step, out: out + apply(second_v(step), khi[i, step], klo[i, step]))
         hand_out(columns, partial, part2, give2)
-        if i == 0:
+        if i == len(order) - 1:
             w_line.arrived()
         for k in columns:
             curved = curved + direct(tline[k], wline[k]) * part2[nc + k]
@@ -336,10 +344,10 @@
                 pltpu.VMEM((nr, rhs, lanes), f32),
                 pltpu.VMEM((nc, rhs, lanes), f32),
                 pltpu.VMEM((2 * nc, rhs, lanes), f32),
-                pltpu.VMEM((nr, rhs + 8, lanes), f32),
+                pltpu.VMEM((nr, rhs, lanes), f32),
                 pltpu.VMEM((nc, rhs, lanes), f32),
                 pltpu.VMEM((2 * nc, rhs, lanes), f32),
-                pltpu.VMEM((nc, 1, lanes), f32),
+                pltpu.VMEM((every, 1, lanes), f32),
                 pltpu.VMEM((every, 1, lanes), f32),
                 pltpu.VMEM(tiles, jnp.bfloat16),
                 pltpu.VMEM(tiles, jnp.bfloat16),
@@ -347,6 +355,7 @@
                 dma((5,)),
                 dma((10,)),
                 dma((10,)),
+                dma((nc,)),
             ],
             compiler_params=pltpu.CompilerParams(
                 collective_id=0, has_side_effects=True, vmem_limit_bytes=56 * 1024 * 1024

time: 24.7 us -> 24.4 us (0.988)
  Pallas kernels: 23.3 us -> 23 us
    pallas_call x1, Pallas kernels: 23.3 us -> 23 us  [on_device(): pl.pallas_call(functools.partial(kernel, nr, nc, feats, rhs, lanes), out_...]
where the time goes in v7:
time: 24.4 us; the launch traced here: 24.2 us
  Pallas kernels  23 us (94%)
  between operations  0.64 us (3%)
  other arithmetic  0.61 us (2%)
    pallas_call x1, Pallas kernels, on_device(): pl.pallas_call(functools.partial(kernel, nr, nc, feats, rhs, lanes), out_...  23 us
    sub x1, other arithmetic, on_device(): return (base + step * along, kept - step * image)  0.61 us

profile of v7, /device:TPU:0, one launch (start us, length us, event | category | flops | bytes accessed | tf_op | source)
XLA Modules:
  0.0 24.2 jit_solution(8747300289287623072)
XLA Ops:
  0.6 23.0 %shard_map.59 = (f32[16,128]{1,0:T(8,128)S(1)}, f32[16,128]{1,0:T(8,128)S(1)}, f32[16,128]{1,0:T(8,128)S(1)}, f32[16,128]{1,0:T(8,128)S(1)}, f32[16,128]{1,0:T(8,128)S(1)}) custom-call(f32[8,128]{1,0:T(8,128)} %points_ref.1, f32[8]{0:T(128)} %scale_in.1, f32[16,128]{1,0:T(8,128)} %targets_ref.1, f32[16]{0:T(128)} %noise_in.1), custom_call_target="tpu_custom_call" | custom-call | tf_op jit(solution)/shard_map/pallas_call | solution.py:333
  23.6 0.6 %multiply_subtract_fusion = (f32[16,128]{1,0:T(8,128)}, f32[16,128]{1,0:T(8,128)}) fusion(f32[16,128]{1,0:T(8,128)S(1)} %get-tuple-element.10, f32[16,128]{1,0:T(8,128)S(1)} %get-tuple-element.8, f32[16,128]{1,0:T(8,128)S(1)} %get-tuple-element.11, f32[16,128]{1,0:T(8,128)S(1)} %get-tuple-element.7, f32[16,128]{1,0:T(8,128)S(1)} %get-tuple-element.9), kind=kLoop, calls=%fused_computation | loop fusion | flops 8192 | bytes 57344 | tf_op jit(solution)/shard_map/sub | solution.py:364

commit v8 on v7

--- a/solution.py
+++ b/solution.py
@@ -12,9 +12,9 @@
 ROOT = math.sqrt(1.0 / math.log(2.0))
 
 
-def loop(low, high, body):
+def loop(low, high, body, key=None):
     if high - low <= 32:
-        for k in range(low, high):
+        for k in sorted(range(low, high), key=key or (lambda k: -k)):
             body(k)
     else:
 
@@ -78,21 +78,32 @@
     r, c = lax.axis_index("row"), lax.axis_index("col")
     every = nr * nc
 
-    def turn(position, k, count):
+    def partner(position, k, count):
+        if isinstance(k, int) and count & (count - 1) == 0:
+            other, bit = position, 1
+            while bit < count:
+                if k & bit:
+                    other = other + bit * (1 - 2 * lax.rem(lax.div(position, bit), 2))
+                bit *= 2
+            return other
         moved = position + k
         return jnp.where(moved >= count, moved - count, moved)
 
-    rows = [r] + [turn(r, k, nr) for k in range(1, nr)] if every <= 32 else None
-    cols = [c] + [turn(c, k, nc) for k in range(1, nc)] if every <= 32 else None
+    rows = [partner(r, k, nr) for k in range(nr)] if every <= 32 else None
+    cols = [partner(c, k, nc) for k in range(nc)] if every <= 32 else None
 
     def at(kr, kc):
         if rows is not None:
             return (rows[kr], cols[kc])
-        return (turn(r, kr, nr), turn(c, kc, nc))
+        return (partner(r, kr, nr), partner(c, kc, nc))
+
+    def distance(k):
+        kr, kc = k // nc, k % nc
+        return kc + bin(kr // 2).count("1") + 0.5 * (kr % 2)
 
     barrier = pltpu.get_barrier_semaphore()
+    loop(1, nc, lambda k: pl.semaphore_signal(barrier, inc=1, device_id=at(0, k), device_id_type=MESH))
     loop(1, nr, lambda k: pl.semaphore_signal(barrier, inc=1, device_id=at(k, 0), device_id_type=MESH))
-    loop(1, nc, lambda k: pl.semaphore_signal(barrier, inc=1, device_id=at(0, k), device_id_type=MESH))
     loads = [
         pltpu.make_async_copy(src, dst, load_sem.at[i])
         for i, (src, dst) in enumerate([
@@ -114,9 +125,9 @@
     class Group:
         count = 0
 
-        def __init__(self, ref, last, peer, src=lambda k: 0, slot_sems=None):
+        def __init__(self, ref, last, peer, src=lambda k: 0, slot_sems=None, key=None):
             self.ref, self.last, self.peer, self.src = ref, last, peer, src
-            self.slot_sems = slot_sems
+            self.slot_sems, self.key = slot_sems, key
             self.sem = Group.count
             Group.count += 1
 
@@ -129,7 +140,7 @@
                     device_id=self.peer(k), device_id_type=MESH,
                 ).start()
 
-            loop(low, self.last if high is None else high, one)
+            loop(low, self.last if high is None else high, one, self.key)
 
         def wait(self, sem):
             slots = self.ref.at[pl.ds(1, self.last - 1)]
@@ -144,18 +155,9 @@
         def sent(self):
             self.wait(send_sem)
 
-    def across_col(k):
-        other, bit = c, 1
-        while bit < nc:
-            if k & bit:
-                other = other + bit * (1 - 2 * lax.rem(lax.div(c, bit), 2))
-            bit *= 2
-        return (r, other)
-
-    paired = nc & (nc - 1) == 0
-    along_col = across_col if paired else lambda k: at(0, k)
+    along_col = lambda k: at(0, k)
     along_row = lambda k: at(k, 0)
-    back_col = across_col if paired else lambda k: at(0, nc - k)
+    back_col = lambda k: at(0, k if nc & (nc - 1) == 0 else nc - k)
     anywhere = lambda k: at(k // nc, k % nc)
     z_line = Group(zline, nc, along_col, slot_sems=line_sem)
     z_plane = Group(zplane, nr, along_row)
@@ -164,9 +166,9 @@
     give = Group(part, nc, back_col, lambda k: nc + k)
     w_line = Group(wline, nc, along_col)
     w_plane = Group(wplane, nr, along_row)
-    scalars = Group(early, every, anywhere)
+    scalars = Group(early, every, anywhere, key=lambda k: -distance(k))
     give2 = Group(part2, nc, back_col, lambda k: nc + k)
-    scalars2 = Group(tiny, every, anywhere)
+    scalars2 = Group(tiny, every, anywhere, key=lambda k: -distance(k))
 
     z_line.start()
     z_plane.start()

time: 24.4 us -> 24.3 us (level)
  no operation moved by 1% of the time
where the time goes in v8:
time: 24.3 us; the launch traced here: 24.1 us
  Pallas kernels  22.8 us (94%)
  between operations  0.64 us (3%)
  other arithmetic  0.61 us (3%)
    pallas_call x1, Pallas kernels, on_device(): pl.pallas_call(functools.partial(kernel, nr, nc, feats, rhs, lanes), out_...  22.8 us
    sub x1, other arithmetic, on_device(): return (base + step * along, kept - step * image)  0.61 us

profile of v8, /device:TPU:0, one launch (start us, length us, event | category | flops | bytes accessed | tf_op | source)
XLA Modules:
  0.0 24.1 jit_solution(885845637408044054)
XLA Ops:
  0.6 22.8 %shard_map.59 = (f32[16,128]{1,0:T(8,128)S(1)}, f32[16,128]{1,0:T(8,128)S(1)}, f32[16,128]{1,0:T(8,128)S(1)}, f32[16,128]{1,0:T(8,128)S(1)}, f32[16,128]{1,0:T(8,128)S(1)}) custom-call(f32[8,128]{1,0:T(8,128)} %points_ref.1, f32[8]{0:T(128)} %scale_in.1, f32[16,128]{1,0:T(8,128)} %targets_ref.1, f32[16]{0:T(128)} %noise_in.1), custom_call_target="tpu_custom_call" | custom-call | tf_op jit(solution)/shard_map/pallas_call | solution.py:335
  23.5 0.6 %multiply_subtract_fusion = (f32[16,128]{1,0:T(8,128)}, f32[16,128]{1,0:T(8,128)}) fusion(f32[16,128]{1,0:T(8,128)S(1)} %get-tuple-element.10, f32[16,128]{1,0:T(8,128)S(1)} %get-tuple-element.8, f32[16,128]{1,0:T(8,128)S(1)} %get-tuple-element.11, f32[16,128]{1,0:T(8,128)S(1)} %get-tuple-element.7, f32[16,128]{1,0:T(8,128)S(1)} %get-tuple-element.9), kind=kLoop, calls=%fused_computation | loop fusion | flops 8192 | bytes 57344 | tf_op jit(solution)/shard_map/sub | solution.py:366

commit v9 on v8

--- a/solution.py
+++ b/solution.py
@@ -72,8 +72,8 @@
     nr, nc, feats, rhs, lanes,
     points_ref, scale_in, targets_ref, noise_in,
     base_ref, step_ref, along_ref, kept_ref, image_ref,
-    raw, scale_ref, noise_ref, zplane, zline, tplane, tline, part, wplane, wline, part2, early, tiny, khi, klo, held,
-    load_sem, send_sem, recv_sem, line_sem,
+    raw, scale_ref, noise_ref, zplane, tplane, line, part, wplane, wline, part2, early, tiny, khi, klo, held,
+    load_sem, send_sem, recv_sem, line_sem, line_send,
 ):
     r, c = lax.axis_index("row"), lax.axis_index("col")
     every = nr * nc
@@ -102,13 +102,20 @@
         return kc + bin(kr // 2).count("1") + 0.5 * (kr % 2)
 
     barrier = pltpu.get_barrier_semaphore()
-    loop(1, nc, lambda k: pl.semaphore_signal(barrier, inc=1, device_id=at(0, k), device_id_type=MESH))
+    top = nc - 1
+
+    def enter(col):
+        pl.semaphore_signal(barrier, inc=1, device_id=(r, col), device_id_type=MESH)
+
+    pl.when(c > 0)(lambda: enter(c - 1))
+    for d in range(top, 0, -1):
+        pl.when(c + d < nc)(lambda d=d: enter(c + d))
     loop(1, nr, lambda k: pl.semaphore_signal(barrier, inc=1, device_id=at(k, 0), device_id_type=MESH))
     loads = [
         pltpu.make_async_copy(src, dst, load_sem.at[i])
         for i, (src, dst) in enumerate([
             (points_ref, raw), (scale_in, scale_ref), (targets_ref, tplane.at[0]),
-            (targets_ref, tline.at[0]), (noise_in, noise_ref),
+            (targets_ref, line.at[c, pl.ds(feats, rhs)]), (noise_in, noise_ref),
         ])
     ]
     for load in loads:
@@ -117,10 +124,10 @@
     loads[1].wait()
     scaled = raw[...] * column(scale_ref, feats, lanes)
     zplane[0] = scaled
-    zline[0] = scaled
+    line[c, 0:feats, :] = scaled
     for load in loads[2:]:
         load.wait()
-    pl.semaphore_wait(barrier, nr + nc - 2)
+    pl.semaphore_wait(barrier, nr - 1 + c + jnp.where(c < top, 1, 0))
 
     class Group:
         count = 0
@@ -159,21 +166,38 @@
     along_row = lambda k: at(k, 0)
     back_col = lambda k: at(0, k if nc & (nc - 1) == 0 else nc - k)
     anywhere = lambda k: at(k // nc, k % nc)
-    z_line = Group(zline, nc, along_col, slot_sems=line_sem)
     z_plane = Group(zplane, nr, along_row)
-    t_line = Group(tline, nc, along_col)
     t_plane = Group(tplane, nr, along_row)
-    give = Group(part, nc, back_col, lambda k: nc + k)
-    w_line = Group(wline, nc, along_col)
+    give = Group(part, nc, along_col, lambda k: nc + k)
+    w_line = Group(wline, nc, back_col)
     w_plane = Group(wplane, nr, along_row)
     scalars = Group(early, every, anywhere, key=lambda k: -distance(k))
-    give2 = Group(part2, nc, back_col, lambda k: nc + k)
+    give2 = Group(part2, nc, along_col, lambda k: nc + k)
     scalars2 = Group(tiny, every, anywhere, key=lambda k: -distance(k))
 
-    z_line.start()
+    def hop(source, col, slot):
+        return pltpu.make_async_remote_copy(
+            src_ref=line.at[source], dst_ref=line.at[source], send_sem=line_send.at[slot],
+            recv_sem=line_sem.at[source], device_id=(r, col), device_id_type=MESH,
+        )
+
+    def landed(source):
+        pltpu.make_async_copy(line.at[source], line.at[source], line_sem.at[source]).wait()
+
+    def pass_on(d):
+        landed(c - d)
+        hop(c - d, c + 1, d).start()
+
+    pl.when(c < top)(lambda: hop(c, c + 1, 0).start())
+    for d in range(top, 0, -1):
+        pl.when(c >= d)(lambda d=d: hop(c, c - d, nc + d).start())
     z_plane.start()
     t_plane.start()
-    t_line.start()
+    for d in range(1, nc):
+        pl.when((c >= d) & (c < top))(lambda d=d: pass_on(d))
+
+    def col_of(k):
+        return at(0, k)[1]
 
     pair = 2 if nr % 2 == 0 else 1
     steps = nr // pair
@@ -241,8 +265,9 @@
     for i, columns in enumerate(order):
         for k in columns:
             if k:
-                z_line.wait_slot(k)
-        right = factors(jnp.concatenate([zline[k] for k in columns], axis=1), False).astype(jnp.bfloat16)
+                source = col_of(k)
+                pl.when((source > c) | (c == top))(lambda source=source: landed(source))
+        right = factors(jnp.concatenate([line[col_of(k), 0:feats, :] for k in columns], axis=1), False).astype(jnp.bfloat16)
         if few and i == 0:
             for step in range(steps):
                 make_tile(i, right, step)
@@ -254,10 +279,9 @@
             partial = total(lambda step, out: first(i, step, out, make_tile(i, right, step)))
         hand_out(columns, partial, part, give)
     target = tplane[0]
-    t_line.arrived()
     along, squared = jnp.zeros((rhs, lanes), jnp.float32), jnp.zeros((rhs, lanes), jnp.float32)
     for k in range(nc):
-        along = along + tline[k] * part[nc + k]
+        along = along + line[col_of(k), feats : feats + rhs, :] * part[nc + k]
         squared = squared + part[nc + k] * part[nc + k]
     early[0] = lane_sums([along, squared, target * target])
     scalars.start()
@@ -299,7 +323,7 @@
         if i == len(order) - 1:
             w_line.arrived()
         for k in columns:
-            curved = curved + direct(tline[k], wline[k]) * part2[nc + k]
+            curved = curved + direct(line[col_of(k), feats : feats + rhs, :], wline[k]) * part2[nc + k]
     tiny[0] = lane_sums([curved, residual * residual, direction * image])
     scalars2.start()
     base_ref[...] = alpha * target
@@ -315,8 +339,12 @@
     step_ref[...] = norm / (curvature + 2.0 * missed * mixed + missed * missed * tw)
     along_ref[...] = direction + missed * target
     image_ref[...] = image2 + missed * image
-    for g in (z_line, z_plane, t_plane, t_line, give, w_line, w_plane, scalars, give2, scalars2):
+    for g in (z_plane, t_plane, give, w_line, w_plane, scalars, give2, scalars2):
         g.sent()
+    pl.when(c < top)(lambda: hop(c, c + 1, 0).wait_send())
+    for d in range(1, nc):
+        pl.when((c >= d) & (c < top))(lambda d=d: hop(c - d, c + 1, d).wait_send())
+        pl.when(c >= d)(lambda d=d: hop(c, c - d, nc + d).wait_send())
 
 
 def solution(mesh):
@@ -342,9 +370,8 @@
                 pltpu.SMEM((feats,), f32),
                 pltpu.SMEM((rhs,), f32),
                 pltpu.VMEM((nr, feats, lanes), f32),
-                pltpu.VMEM((nc, feats, lanes), f32),
                 pltpu.VMEM((nr, rhs, lanes), f32),
-                pltpu.VMEM((nc, rhs, lanes), f32),
+                pltpu.VMEM((nc, feats + rhs, lanes), f32),
                 pltpu.VMEM((2 * nc, rhs, lanes), f32),
                 pltpu.VMEM((nr, rhs, lanes), f32),
                 pltpu.VMEM((nc, rhs, lanes), f32),
@@ -358,6 +385,7 @@
                 dma((10,)),
                 dma((10,)),
                 dma((nc,)),
+                dma((2 * nc,)),
             ],
             compiler_params=pltpu.CompilerParams(
                 collective_id=0, has_side_effects=True, vmem_limit_bytes=56 * 1024 * 1024

time: 24.3 us -> 26.7 us (1.099)
  Pallas kernels: 22.8 us -> 25.3 us
    pallas_call x1, Pallas kernels: 22.8 us -> 25.3 us  [on_device(): pl.pallas_call(functools.partial(kernel, nr, nc, feats, rhs, lanes), out_...]
where the time goes in v9:
time: 26.7 us; the launch traced here: 26.5 us
  Pallas kernels  25.3 us (95%)
  between operations  0.64 us (2%)
  other arithmetic  0.61 us (2%)
    pallas_call x1, Pallas kernels, on_device(): pl.pallas_call(functools.partial(kernel, nr, nc, feats, rhs, lanes), out_...  25.3 us
    sub x1, other arithmetic, on_device(): return (base + step * along, kept - step * image)  0.61 us

profile of v9, /device:TPU:0, one launch (start us, length us, event | category | flops | bytes accessed | tf_op | source)
XLA Modules:
  0.0 26.5 jit_solution(119283705956468763)
XLA Ops:
  0.6 25.3 %shard_map.59 = (f32[16,128]{1,0:T(8,128)S(1)}, f32[16,128]{1,0:T(8,128)S(1)}, f32[16,128]{1,0:T(8,128)S(1)}, f32[16,128]{1,0:T(8,128)S(1)}, f32[16,128]{1,0:T(8,128)S(1)}) custom-call(f32[8,128]{1,0:T(8,128)} %points_ref.1, f32[8]{0:T(128)} %scale_in.1, f32[16,128]{1,0:T(8,128)} %targets_ref.1, f32[16]{0:T(128)} %noise_in.1), custom_call_target="tpu_custom_call" | custom-call | tf_op jit(solution)/shard_map/pallas_call | solution.py:363
  25.9 0.6 %multiply_subtract_fusion = (f32[16,128]{1,0:T(8,128)}, f32[16,128]{1,0:T(8,128)}) fusion(f32[16,128]{1,0:T(8,128)S(1)} %get-tuple-element.10, f32[16,128]{1,0:T(8,128)S(1)} %get-tuple-element.8, f32[16,128]{1,0:T(8,128)S(1)} %get-tuple-element.11, f32[16,128]{1,0:T(8,128)S(1)} %get-tuple-element.7, f32[16,128]{1,0:T(8,128)S(1)} %get-tuple-element.9), kind=kLoop, calls=%fused_computation | loop fusion | flops 8192 | bytes 57344 | tf_op jit(solution)/shard_map/sub | solution.py:394

commit v10 on v8

--- a/solution.py
+++ b/solution.py
@@ -177,7 +177,7 @@
 
     pair = 2 if nr % 2 == 0 else 1
     steps = nr // pair
-    wide = 2 if nc % 2 == 0 else 1
+    wide = math.gcd(nc, 4)
     order = [list(range(i, i + wide)) for i in range(0, nc, wide)]
     few = steps <= FEW
 
@@ -326,7 +326,7 @@
         feats, lanes = points.shape
         rhs = targets.shape[0]
         pair = 2 if nr % 2 == 0 else 1
-        wide = 2 if nc % 2 == 0 else 1
+        wide = math.gcd(nc, 4)
         every = nr * nc
         f32 = jnp.float32
         dma = pltpu.SemaphoreType.DMA

time: 24.3 us -> 23.9 us (0.984)
  Pallas kernels: 22.8 us -> 22.5 us
    pallas_call x1, Pallas kernels: 22.8 us -> 22.5 us  [on_device(): pl.pallas_call(functools.partial(kernel, nr, nc, feats, rhs, lanes), out_...]
where the time goes in v10:
time: 23.9 us; the launch traced here: 23.7 us
  Pallas kernels  22.5 us (94%)
  between operations  0.64 us (3%)
  other arithmetic  0.61 us (3%)
    pallas_call x1, Pallas kernels, on_device(): pl.pallas_call(functools.partial(kernel, nr, nc, feats, rhs, lanes), out_...  22.5 us
    sub x1, other arithmetic, on_device(): return (base + step * along, kept - step * image)  0.61 us

profile of v10, /device:TPU:0, one launch (start us, length us, event | category | flops | bytes accessed | tf_op | source)
XLA Modules:
  0.0 23.7 jit_solution(12774067311602366454)
XLA Ops:
  0.6 22.5 %shard_map.59 = (f32[16,128]{1,0:T(8,128)S(1)}, f32[16,128]{1,0:T(8,128)S(1)}, f32[16,128]{1,0:T(8,128)S(1)}, f32[16,128]{1,0:T(8,128)S(1)}, f32[16,128]{1,0:T(8,128)S(1)}) custom-call(f32[8,128]{1,0:T(8,128)} %points_ref.1, f32[8]{0:T(128)} %scale_in.1, f32[16,128]{1,0:T(8,128)} %targets_ref.1, f32[16]{0:T(128)} %noise_in.1), custom_call_target="tpu_custom_call" | custom-call | tf_op jit(solution)/shard_map/pallas_call | solution.py:335
  23.1 0.6 %multiply_subtract_fusion = (f32[16,128]{1,0:T(8,128)}, f32[16,128]{1,0:T(8,128)}) fusion(f32[16,128]{1,0:T(8,128)S(1)} %get-tuple-element.10, f32[16,128]{1,0:T(8,128)S(1)} %get-tuple-element.8, f32[16,128]{1,0:T(8,128)S(1)} %get-tuple-element.11, f32[16,128]{1,0:T(8,128)S(1)} %get-tuple-element.7, f32[16,128]{1,0:T(8,128)S(1)} %get-tuple-element.9), kind=kLoop, calls=%fused_computation | loop fusion | flops 8192 | bytes 57344 | tf_op jit(solution)/shard_map/sub | solution.py:366

commit v11 on v10

--- a/solution.py
+++ b/solution.py
@@ -261,10 +261,6 @@
         squared = squared + part[nc + k] * part[nc + k]
     early[0] = lane_sums([along, squared, target * target])
     scalars.start()
-    if few:
-        for i in range(len(order)):
-            for step in range(steps):
-                klo[i, step] = low_part(held[i, step])
 
     noise = column(noise_ref, rhs, lanes)
     image = part[nc] + noise * target
@@ -276,6 +272,10 @@
     wline[0] = image
     w_plane.start()
     w_line.start()
+    if few:
+        for i in range(len(order)):
+            for step in range(steps):
+                klo[i, step] = low_part(held[i, step])
     scalars.arrived()
     sums = to_column(jnp.sum(early[...], axis=0))
     tkt, spread, tt = sums[:rhs], sums[rhs : 2 * rhs], sums[2 * rhs : 3 * rhs]

time: 23.9 us -> 24 us (level)
  no operation moved by 1% of the time
where the time goes in v11:
time: 24 us; the launch traced here: 23.8 us
  Pallas kernels  22.6 us (94%)
  between operations  0.64 us (3%)
  other arithmetic  0.61 us (3%)
    pallas_call x1, Pallas kernels, on_device(): pl.pallas_call(functools.partial(kernel, nr, nc, feats, rhs, lanes), out_...  22.6 us
    sub x1, other arithmetic, on_device(): return (base + step * along, kept - step * image)  0.61 us

profile of v11, /device:TPU:0, one launch (start us, length us, event | category | flops | bytes accessed | tf_op | source)
XLA Modules:
  0.0 23.8 jit_solution(12907005448224985059)
XLA Ops:
  0.6 22.6 %shard_map.59 = (f32[16,128]{1,0:T(8,128)S(1)}, f32[16,128]{1,0:T(8,128)S(1)}, f32[16,128]{1,0:T(8,128)S(1)}, f32[16,128]{1,0:T(8,128)S(1)}, f32[16,128]{1,0:T(8,128)S(1)}) custom-call(f32[8,128]{1,0:T(8,128)} %points_ref.1, f32[8]{0:T(128)} %scale_in.1, f32[16,128]{1,0:T(8,128)} %targets_ref.1, f32[16]{0:T(128)} %noise_in.1), custom_call_target="tpu_custom_call" | custom-call | tf_op jit(solution)/shard_map/pallas_call | solution.py:335
  23.2 0.6 %multiply_subtract_fusion = (f32[16,128]{1,0:T(8,128)}, f32[16,128]{1,0:T(8,128)}) fusion(f32[16,128]{1,0:T(8,128)S(1)} %get-tuple-element.10, f32[16,128]{1,0:T(8,128)S(1)} %get-tuple-element.8, f32[16,128]{1,0:T(8,128)S(1)} %get-tuple-element.11, f32[16,128]{1,0:T(8,128)S(1)} %get-tuple-element.7, f32[16,128]{1,0:T(8,128)S(1)} %get-tuple-element.9), kind=kLoop, calls=%fused_computation | loop fusion | flops 8192 | bytes 57344 | tf_op jit(solution)/shard_map/sub | solution.py:366
